TPU v7x, 32 devices: a whole 2x2x4 slice. The times are simulated.
32 devices in a mesh: batch: 16 (over z, x, core), seq: 2 (over y).
Axes of the slice: x: 2, y: 2, z: 4, core: 2. Of those that a mesh axis runs over, the one named last changes fastest.
Arguments:
- tokens: bfloat16 [16, 2048, 768], P('batch', 'seq'), may hold values from -6 to 6
- cotangent: bfloat16 [16, 2048, 768], P('batch', 'seq'), may hold values from -6 to 6
- segments: int32 [16, 2048], P('batch'), may hold values from 0 to 3, as said below
- adapter_index: int32 [16, 1], P('batch'), may hold values from 0 to 3
- qkv_weight: bfloat16 [1, 3, 768, 768], P(None, None, ('batch', 'seq')), may hold values from -0.21875 to 0.21875
- out_weight: bfloat16 [1, 768, 768], P(None, ('batch', 'seq')), may hold values from -0.875 to 0.875
- ffn_in_weight: bfloat16 [1, 2, 768, 3072], P(None, None, ('batch', 'seq')), may hold values from -0.21875 to 0.21875
- ffn_out_weight: bfloat16 [1, 3072, 768], P(None, ('batch', 'seq')), may hold values from -0.109375 to 0.109375
- norm_gain: float32 [1, 2, 768], replicated, may hold values from 0.1 to 1.9
- norm_bias: float32 [1, 2, 768], replicated, may hold values from -2 to 2
- adapt_in: bfloat16 [1, 4, 6, 768, 16], replicated, may hold values from -0.21875 to 0.21875
- adapt_down: bfloat16 [1, 4, 3072, 16], replicated, may hold values from -0.109375 to 0.109375
- adapt_out: bfloat16 [1, 4, 5, 16, 768], replicated, may hold values from -1.5 to 1.5
- adapt_ffn: bfloat16 [1, 4, 2, 16, 3072], replicated, may hold values from -1.5 to 1.5
Outputs:
- mixed: bfloat16 [16, 2048, 768], P('batch', 'seq')
- input_grad: bfloat16 [16, 2048, 768], P('batch', 'seq')
- grad_adapt_in: float32 [1, 4, 6, 768, 16], replicated
- grad_adapt_down: float32 [1, 4, 3072, 16], replicated
- grad_adapt_out: float32 [1, 4, 5, 16, 768], replicated
- grad_adapt_ffn: float32 [1, 4, 2, 16, 3072], replicated
Inputs may be any that keep to these rules, and one draw needn't show every extreme that they name: `segments`: document numbers start at 0 in each sequence and rise by one at each new document; every sequence holds exactly 4 documents, one of which starts before position 1024 and ends at or after position 1024. `adapter_index`: every adapter is used by some sequence.
All inputs are finite; a program needn't handle non-finite values.
Results may differ from a plain program's by a relative error of at most 0.023.
The roundings to bfloat16 on the way count: a program that leaves them out, or rounds other values in their place, can miss the bound.
Values may be sent and summed in bfloat16 or wider, within the bound.
A program may use at most 320 MiB of HBM per device.

v0:
```python
import functools
import math

import jax
import jax.numpy as jnp
from jax import lax
from jax.experimental import pallas as pl
from jax.experimental.pallas import tpu as pltpu
from jax.sharding import PartitionSpec as P

HEADS = 12
HEAD_DIM = 64
ADAPTERS = 4
LAYERS = 1
HALF = 512
D = HEADS * HEAD_DIM
FF = 4 * D


EPSILON = 1e-06
ROPE_BASE = 1000.0
PRECISE = lax.Precision.HIGHEST


def shifted(array, axis, by):
    count = lax.axis_size(axis)
    pairs = [(i, i + by) for i in range(count) if 0 <= i + by < count]
    return lax.ppermute(array, axis, pairs)


def doc_positions(segment_ids):
    position_ids = jnp.arange(segment_ids.shape[-1], dtype=jnp.int32)
    starts_here = jnp.concatenate(
        [
            jnp.ones(segment_ids.shape[:-1] + (1,), dtype=jnp.bool_),
            segment_ids[..., 1:] != segment_ids[..., :-1],
        ],
        axis=-1,
    )
    doc_start = lax.cummax(jnp.where(starts_here, position_ids, 0), axis=segment_ids.ndim - 1)
    return (position_ids - doc_start).astype(jnp.float32)


def rope_tables(segment_ids):
    positions = doc_positions(segment_ids)
    frequency = jnp.power(ROPE_BASE, -2.0 * jnp.arange(HEAD_DIM // 2, dtype=jnp.float32) / HEAD_DIM)
    angles = positions[..., None] * frequency
    return (jnp.cos(angles), jnp.sin(angles))


def rotate(vectors, cosine_table, sine_table):
    half_dim = vectors.shape[-1] // 2
    first_half = vectors[..., :half_dim]
    second_half = vectors[..., half_dim:]
    cosine_rows = cosine_table[..., None, :]
    sine_rows = sine_table[..., None, :]
    return jnp.concatenate(
        [
            first_half * cosine_rows - second_half * sine_rows,
            second_half * cosine_rows + first_half * sine_rows,
        ],
        axis=-1,
    )


def norm_apply(residual, gain_row, bias_row):
    centre = residual - jnp.mean(residual, axis=-1, keepdims=True)
    spread = jnp.mean(centre * centre, axis=-1, keepdims=True)
    return centre * lax.rsqrt(spread + EPSILON) * gain_row + bias_row


def split_heads(merged, group_count):
    seqs_here, row_count, _ = merged.shape
    return merged.reshape(seqs_here, row_count, group_count, -1, HEAD_DIM).transpose(2, 0, 1, 3, 4)


def join_heads(grouped):
    group_count, seqs_here, row_count, heads_group, head_size = grouped.shape
    return grouped.transpose(1, 2, 0, 3, 4).reshape(
        seqs_here, row_count, group_count * heads_group * head_size
    )


def shards(
    tokens,
    cotangent,
    segments,
    adapter_index,
    qkv_weight,
    out_weight,
    ffn_in_weight,
    ffn_out_weight,
    norm_gain,
    norm_bias,
    adapt_in,
    adapt_down,
    adapt_out,
    adapt_ffn,
):
    seqs_here, tok_rows, model_width = tokens.shape
    heads_group = math.gcd(HEADS, 4)
    group_count = HEADS // heads_group
    score_scale = 1.0 / math.sqrt(HEAD_DIM)
    seq_count = lax.axis_size("seq")
    row_base = lax.axis_index("seq") * tok_rows
    shift_plan = []
    for distance in range(1, min(seq_count, HALF // tok_rows + 2)):
        row_count = min(tok_rows, HALF - (distance - 1) * tok_rows)
        if row_count > 0:
            shift_plan.append((distance, row_count))
            shift_plan.append((-distance, row_count))
    left_total = sum((plan_item[1] for plan_item in shift_plan if plan_item[0] > 0))
    key_rows = 2 * left_total + tok_rows
    key_places = {}
    passed_rows = 0
    for distance, row_count in shift_plan:
        if distance > 0:
            key_places[distance] = left_total - passed_rows - row_count
            key_places[-distance] = left_total + tok_rows + passed_rows
            passed_rows += row_count
    cosine_all, sine_all = rope_tables(segments)
    cosine_here = lax.dynamic_slice_in_dim(cosine_all, row_base, tok_rows, 1)
    sine_here = lax.dynamic_slice_in_dim(sine_all, row_base, tok_rows, 1)
    padded_ids = jnp.pad(segments, ((0, 0), (HALF, HALF)), constant_values=-1)
    key_ids = lax.dynamic_slice_in_dim(padded_ids, row_base - left_total + HALF, key_rows, 1)
    query_ids = lax.dynamic_slice_in_dim(segments, row_base, tok_rows, 1)
    offsets = (
        jnp.arange(tok_rows, dtype=jnp.int32)[:, None]
        - jnp.arange(key_rows, dtype=jnp.int32)[None, :]
        + left_total
    )
    visible = (query_ids[:, :, None] == key_ids[:, None, :]) & (jnp.abs(offsets) <= HALF)[None]
    slot_hits = adapter_index[:, 0][:, None] == jnp.arange(ADAPTERS, dtype=jnp.int32)[None, :]
    slot_low = slot_hits.astype(jnp.bfloat16)
    slot_full = slot_hits.astype(jnp.float32)

    def select_adapter(table):
        return jnp.einsum(
            "se,le...->ls...", slot_low, table, preferred_element_type=jnp.float32
        ).astype(jnp.bfloat16)

    def spread_slots(per_sequence):
        return jnp.einsum("se,s...->e...", slot_full, per_sequence, precision=PRECISE)

    chosen_in = select_adapter(adapt_in)
    chosen_down = select_adapter(adapt_down)
    chosen_out = select_adapter(adapt_out)
    chosen_ffn = select_adapter(adapt_ffn)

    def forward_group(items):
        query_block, key_block, value_block = items
        scores = (
            jnp.einsum(
                "sqhd,skhd->shqk", query_block, key_block, preferred_element_type=jnp.float32
            )
            * score_scale
        )
        scores = jnp.where(visible[:, None], scores, -1e30)
        biggest = jnp.max(scores, axis=-1, keepdims=True)
        lifted = jnp.exp(scores - biggest)
        row_total = jnp.sum(lifted, axis=-1, keepdims=True)
        probability = (lifted / row_total).astype(jnp.bfloat16)
        result = jnp.einsum(
            "shqk,skhd->sqhd", probability, value_block, preferred_element_type=jnp.float32
        )
        return (result.astype(jnp.bfloat16), (biggest + jnp.log(row_total))[..., 0])

    def backward_group(items):
        query_block, key_block, value_block, grad_block, log_total = items
        scores = (
            jnp.einsum(
                "sqhd,skhd->shqk", query_block, key_block, preferred_element_type=jnp.float32
            )
            * score_scale
        )
        scores = jnp.where(visible[:, None], scores, -1e30)
        probability = jnp.exp(scores - log_total[..., None])
        d_prob = jnp.einsum(
            "sqhd,skhd->shqk", grad_block, value_block, preferred_element_type=jnp.float32
        )
        delta = jnp.sum(probability * d_prob, axis=-1, keepdims=True)
        d_score = (probability * (d_prob - delta)).astype(jnp.bfloat16)
        d_query = (
            jnp.einsum("shqk,skhd->sqhd", d_score, key_block, preferred_element_type=jnp.float32)
            * score_scale
        )
        d_key = (
            jnp.einsum("shqk,sqhd->skhd", d_score, query_block, preferred_element_type=jnp.float32)
            * score_scale
        )
        d_value = jnp.einsum(
            "shqk,sqhd->skhd",
            probability.astype(jnp.bfloat16),
            grad_block,
            preferred_element_type=jnp.float32,
        )
        return (d_query, d_key, d_value)

    state = tokens.astype(jnp.float32)
    layer_index = 0
    w_qkv = lax.all_gather(qkv_weight[layer_index], ("batch", "seq"), axis=1, tiled=True)
    w_out = lax.all_gather(out_weight[layer_index], ("batch", "seq"), axis=0, tiled=True)
    w_in = lax.all_gather(ffn_in_weight[layer_index], ("batch", "seq"), axis=1, tiled=True)
    w_down = lax.all_gather(ffn_out_weight[layer_index], ("batch", "seq"), axis=0, tiled=True)
    held = [(w_qkv, w_out, w_in, w_down)]
    act_one = state.astype(jnp.bfloat16)
    low_qkv = jnp.einsum(
        "std,spdr->pstr",
        act_one,
        chosen_in[layer_index][:, 0:3],
        preferred_element_type=jnp.float32,
    ).astype(jnp.bfloat16)
    proj = jnp.einsum(
        "std,pde->pste", act_one, w_qkv, preferred_element_type=jnp.float32
    ) + jnp.einsum(
        "pstr,spre->pste",
        low_qkv,
        chosen_out[layer_index][:, 0:3],
        preferred_element_type=jnp.float32,
    )
    queries = (
        rotate(proj[0].reshape(seqs_here, tok_rows, HEADS, HEAD_DIM), cosine_here, sine_here)
        .astype(jnp.bfloat16)
        .reshape(seqs_here, tok_rows, model_width)
    )
    key_rot = (
        rotate(proj[1].reshape(seqs_here, tok_rows, HEADS, HEAD_DIM), cosine_here, sine_here)
        .astype(jnp.bfloat16)
        .reshape(seqs_here, tok_rows, model_width)
    )
    key_value = jnp.stack([key_rot, proj[2].astype(jnp.bfloat16)])
    edges = {}
    for step_by, row_count in shift_plan:
        if step_by > 0:
            outgoing = key_value[:, :, tok_rows - row_count :]
        else:
            outgoing = key_value[:, :, :row_count]
        edges[step_by] = shifted(outgoing, "seq", step_by)
    earlier = [edges[distance] for distance, row_count in reversed(shift_plan) if distance > 0]
    later = [edges[-distance] for distance, row_count in shift_plan if distance > 0]
    window = jnp.concatenate(earlier + [key_value] + later, axis=2)
    heads_out, log_total = lax.map(
        forward_group,
        (
            split_heads(queries, group_count),
            split_heads(window[0], group_count),
            split_heads(window[1], group_count),
        ),
    )
    attended = join_heads(heads_out)
    low_out = jnp.einsum(
        "std,sdr->str", attended, chosen_in[layer_index][:, 3], preferred_element_type=jnp.float32
    ).astype(jnp.bfloat16)
    branch = jnp.einsum(
        "std,de->ste", attended, w_out, preferred_element_type=jnp.float32
    ) + jnp.einsum(
        "str,sre->ste", low_out, chosen_out[layer_index][:, 3], preferred_element_type=jnp.float32
    )
    resid_one = state + branch
    hidden = norm_apply(resid_one, norm_gain[layer_index, 0], norm_bias[layer_index, 0])
    act_two = hidden.astype(jnp.bfloat16)
    low_ffn = jnp.einsum(
        "std,spdr->pstr",
        act_two,
        chosen_in[layer_index][:, 4:6],
        preferred_element_type=jnp.float32,
    ).astype(jnp.bfloat16)
    gate_up = jnp.einsum(
        "std,pdf->pstf", act_two, w_in, preferred_element_type=jnp.float32
    ) + jnp.einsum(
        "pstr,sprf->pstf", low_ffn, chosen_ffn[layer_index], preferred_element_type=jnp.float32
    )
    inner = (jax.nn.silu(gate_up[0]) * gate_up[1]).astype(jnp.bfloat16)
    low_down = jnp.einsum(
        "stf,sfr->str", inner, chosen_down[layer_index], preferred_element_type=jnp.float32
    ).astype(jnp.bfloat16)
    branch_two = jnp.einsum(
        "stf,fe->ste", inner, w_down, preferred_element_type=jnp.float32
    ) + jnp.einsum(
        "str,sre->ste", low_down, chosen_out[layer_index][:, 4], preferred_element_type=jnp.float32
    )
    resid_two = hidden + branch_two
    kept = [
        (
            act_one,
            low_qkv,
            queries,
            window,
            log_total,
            attended,
            low_out,
            resid_one,
            act_two,
            low_ffn,
            gate_up,
            inner,
            low_down,
            resid_two,
        )
    ]
    state = norm_apply(resid_two, norm_gain[layer_index, 1], norm_bias[layer_index, 1])
    mixed = state.astype(jnp.bfloat16)
    grad = cotangent.astype(jnp.float32)
    collected = [None] * LAYERS
    for layer_index in reversed(range(LAYERS)):
        (
            act_one,
            low_qkv,
            queries,
            window,
            log_total,
            attended,
            low_out,
            resid_one,
            act_two,
            low_ffn,
            gate_up,
            inner,
            low_down,
            resid_two,
        ) = kept[layer_index]
        w_qkv, w_out, w_in, w_down = held[layer_index]
        gain_two = norm_gain[layer_index, 1]
        bias_two = norm_bias[layer_index, 1]
        _, pull_two = jax.vjp(lambda residual: norm_apply(residual, gain_two, bias_two), resid_two)
        (d_resid_two,) = pull_two(grad)
        d_branch_two = d_resid_two.astype(jnp.bfloat16)
        d_low_down = jnp.einsum(
            "ste,sre->str",
            d_branch_two,
            chosen_out[layer_index][:, 4],
            preferred_element_type=jnp.float32,
        ).astype(jnp.bfloat16)
        g_out_down = jnp.einsum(
            "str,ste->sre", low_down, d_branch_two, preferred_element_type=jnp.float32
        )
        g_down = jnp.einsum("stf,str->sfr", inner, d_low_down, preferred_element_type=jnp.float32)
        d_inner = jnp.einsum(
            "ste,fe->stf", d_branch_two, w_down, preferred_element_type=jnp.float32
        ) + jnp.einsum(
            "str,sfr->stf", d_low_down, chosen_down[layer_index], preferred_element_type=jnp.float32
        )
        _, pull_act = jax.vjp(
            lambda gate_part, up_part: jax.nn.silu(gate_part) * up_part, gate_up[0], gate_up[1]
        )
        d_gate, d_up = pull_act(d_inner)
        d_gate_up = jnp.stack([d_gate, d_up]).astype(jnp.bfloat16)
        d_low_ffn = jnp.einsum(
            "pstf,sprf->pstr",
            d_gate_up,
            chosen_ffn[layer_index],
            preferred_element_type=jnp.float32,
        ).astype(jnp.bfloat16)
        g_ffn = jnp.einsum(
            "pstr,pstf->sprf", low_ffn, d_gate_up, preferred_element_type=jnp.float32
        )
        g_in_ffn = jnp.einsum(
            "std,pstr->spdr", act_two, d_low_ffn, preferred_element_type=jnp.float32
        )
        ffn_in_sum = spread_slots(g_in_ffn)
        ffn_down_sum = spread_slots(g_down)
        ffn_out_sum = spread_slots(g_out_down[:, None])
        ffn_ffn_sum = spread_slots(g_ffn)
        d_hidden = (
            d_resid_two
            + jnp.einsum("pstf,pdf->std", d_gate_up, w_in, preferred_element_type=jnp.float32)
            + jnp.einsum(
                "pstr,spdr->std",
                d_low_ffn,
                chosen_in[layer_index][:, 4:6],
                preferred_element_type=jnp.float32,
            )
        )
        gain_one = norm_gain[layer_index, 0]
        bias_one = norm_bias[layer_index, 0]
        _, pull_one = jax.vjp(lambda residual: norm_apply(residual, gain_one, bias_one), resid_one)
        (d_resid_one,) = pull_one(d_hidden)
        d_branch = d_resid_one.astype(jnp.bfloat16)
        d_low_out = jnp.einsum(
            "ste,sre->str",
            d_branch,
            chosen_out[layer_index][:, 3],
            preferred_element_type=jnp.float32,
        ).astype(jnp.bfloat16)
        g_out_att = jnp.einsum(
            "str,ste->sre", low_out, d_branch, preferred_element_type=jnp.float32
        )
        g_in_att = jnp.einsum(
            "std,str->sdr", attended, d_low_out, preferred_element_type=jnp.float32
        )
        d_attended = (
            jnp.einsum("ste,de->std", d_branch, w_out, preferred_element_type=jnp.float32)
            + jnp.einsum(
                "str,sdr->std",
                d_low_out,
                chosen_in[layer_index][:, 3],
                preferred_element_type=jnp.float32,
            )
        ).astype(jnp.bfloat16)
        d_query_heads, d_key_heads, d_value_heads = lax.map(
            backward_group,
            (
                split_heads(queries, group_count),
                split_heads(window[0], group_count),
                split_heads(window[1], group_count),
                split_heads(d_attended, group_count),
                log_total,
            ),
        )
        d_query = join_heads(d_query_heads)
        d_window = jnp.stack([join_heads(d_key_heads), join_heads(d_value_heads)])
        d_pair = d_window[:, :, left_total : left_total + tok_rows]
        for step_by, row_count in shift_plan:
            returning = lax.slice_in_dim(
                d_window, key_places[step_by], key_places[step_by] + row_count, axis=2
            )
            arrived = shifted(returning.astype(jnp.bfloat16), "seq", -step_by).astype(
                returning.dtype
            )
            if step_by > 0:
                d_pair = d_pair.at[:, :, tok_rows - row_count :].add(arrived)
            else:
                d_pair = d_pair.at[:, :, :row_count].add(arrived)
        d_query_rot = rotate(
            d_query.reshape(seqs_here, tok_rows, HEADS, HEAD_DIM), cosine_here, -sine_here
        ).reshape(seqs_here, tok_rows, model_width)
        d_key_rot = rotate(
            d_pair[0].reshape(seqs_here, tok_rows, HEADS, HEAD_DIM), cosine_here, -sine_here
        ).reshape(seqs_here, tok_rows, model_width)
        d_proj = jnp.stack([d_query_rot, d_key_rot, d_pair[1]]).astype(jnp.bfloat16)
        d_low_qkv = jnp.einsum(
            "pste,spre->pstr",
            d_proj,
            chosen_out[layer_index][:, 0:3],
            preferred_element_type=jnp.float32,
        ).astype(jnp.bfloat16)
        g_out_qkv = jnp.einsum(
            "pstr,pste->spre", low_qkv, d_proj, preferred_element_type=jnp.float32
        )
        g_in_qkv = jnp.einsum(
            "std,pstr->spdr", act_one, d_low_qkv, preferred_element_type=jnp.float32
        )
        grad = (
            d_resid_one
            + jnp.einsum("pste,pde->std", d_proj, w_qkv, preferred_element_type=jnp.float32)
            + jnp.einsum(
                "pstr,spdr->std",
                d_low_qkv,
                chosen_in[layer_index][:, 0:3],
                preferred_element_type=jnp.float32,
            )
        )
        att_in_sum = spread_slots(jnp.concatenate([g_in_qkv, g_in_att[:, None]], axis=1))
        att_out_sum = spread_slots(jnp.concatenate([g_out_qkv, g_out_att[:, None]], axis=1))
        collected[layer_index] = (
            jnp.concatenate([att_in_sum, ffn_in_sum], axis=1),
            ffn_down_sum,
            jnp.concatenate([att_out_sum, ffn_out_sum], axis=1),
            ffn_ffn_sum,
        )
    input_grad = grad.astype(jnp.bfloat16)
    stack_in = jnp.stack([collected[0][0]])
    stack_down = jnp.stack([collected[0][1]])
    stack_out = jnp.stack([collected[0][2]])
    stack_ffn = jnp.stack([collected[0][3]])
    stack_in, stack_down, stack_out, stack_ffn = lax.psum(
        (stack_in, stack_down, stack_out, stack_ffn), ("batch", "seq")
    )
    return (mixed, input_grad, stack_in, stack_down, stack_out, stack_ffn)


MESH = pl.DeviceIdType.MESH
NCHUNK = 10


class Gather:
    def __init__(self, sems, direct=()):
        self.direct = direct
        (
            self.zs, self.zr, self.xs, self.xr, self.ys, self.yr, self.ds, self.dr, self.es, self.er, self.fs, self.fr,
            self.cs, self.cr,
        ) = sems
        b = lax.axis_index("batch")
        self.s = lax.axis_index("seq")
        self.core = lax.rem(b, 2)
        self.x = lax.rem(lax.div(b, 2), 2)
        self.z = lax.div(b, 4)
        self.devx = (b + 2 - 4 * self.x, self.s)
        self.devy = (b, 1 - self.s)
        self.devc = (b + 1 - 2 * self.core, self.s)
        self.pair = self.z + 1 - 2 * lax.rem(self.z, 2)
        self.me = self.owner(self.z, 0, 0, 0)

    def owner(self, z, dx, dy, dc):
        x = 1 - self.x if dx else self.x
        y = 1 - self.s if dy else self.s
        c = 1 - self.core if dc else self.core
        return (z * 4 + x * 2 + c) * 2 + y

    def devz(self, z):
        return (z * 4 + self.x * 2 + self.core, self.s)

    def zof(self, d):
        return lax.rem(self.z + d, 4)

    def copy(self, c, j, half, dev, send, recv):
        v = self.view(c, j, half)
        return pltpu.make_async_remote_copy(v, v, send, recv, device_id=dev, device_id_type=MESH)

    def to_z(self, c, z):
        return self.copy(c, self.me, None, self.devz(z), self.zs.at[c, z], self.zr.at[c, self.z])

    def from_z(self, c, z):
        return self.copy(c, self.owner(z, 0, 0, 0), None, self.devz(z), self.zs.at[c, z], self.zr.at[c, z])

    def on_x(self, c, z, arriving):
        return self.copy(c, self.owner(z, arriving, 0, 0), None, self.devx, self.xs.at[c, z], self.xr.at[c, z])

    def on_y(self, c, z, arriving):
        return self.copy(c, self.owner(z, 0, arriving, 0), None, self.devy, self.ys.at[c, z], self.yr.at[c, z])

    def corner_x(self, c, z, arriving):
        return self.copy(c, self.owner(z, arriving, 1, 0), 0, self.devx, self.ds.at[c, z], self.dr.at[c, z])

    def corner_y(self, c, z, arriving):
        return self.copy(c, self.owner(z, 1, arriving, 0), 1, self.devy, self.es.at[c, z], self.er.at[c, z])

    def corner_z(self, c, z):
        return self.copy(c, self.owner(z, 1, 1, 0), None, self.devz(self.pair), self.fs.at[c, z], self.fr.at[c, z])

    def on_core(self, c, kind, z, arriving):
        j = self.owner(z, kind & 1, kind >> 1, arriving)
        k = kind * 4 + z
        return self.copy(c, j, None, self.devc, self.cs.at[c, k], self.cr.at[c, k])

    def barrier(self):
        bar = pltpu.get_barrier_semaphore()
        for dev in (self.devx, self.devy, self.devc, self.devz(self.zof(1)), self.devz(self.zof(2)), self.devz(self.zof(3))):
            pl.semaphore_signal(bar, inc=1, device_id=dev, device_id_type=MESH)
        pl.semaphore_wait(bar, 6)

    def others(self):
        z = self.z
        first = jnp.where(z == 0, 1, z - 1)
        second = jnp.where(z == 0, 2, jnp.where(z == 3, 1, z + 1))
        third = jnp.where(z <= 1, 3, 0)
        return first, second, third

    def corners(self, c):
        return (0, 1, 2, 3) if c in self.direct else (0, 2)

    def send_z(self, c):
        for z in self.others():
            self.to_z(c, z).start()

    def send_xy(self, c):
        self.on_x(c, self.z, 0).start()
        self.on_y(c, self.z, 0).start()
        self.on_core(c, 0, self.z, 0).start()

    def stage_own(self, c):
        self.send_z(c)
        self.send_xy(c)

    def stage_z(self, c):
        for z in self.others():
            self.from_z(c, z).wait_recv()
            self.on_x(c, z, 0).start()
            self.on_y(c, z, 0).start()
            self.on_core(c, 0, z, 0).start()

    def stage_xy(self, c):
        for d in (0, 2, 1, 3):
            z = self.zof(d)
            self.on_x(c, z, 1).wait_recv()
            if d in self.corners(c):
                self.corner_y(c, z, 0).start()
            self.on_core(c, 1, z, 0).start()
            self.on_y(c, z, 1).wait_recv()
            if d in self.corners(c):
                self.corner_x(c, z, 0).start()
            self.on_core(c, 2, z, 0).start()

    def stage_corner(self, c):
        for d in self.corners(c):
            z = self.zof(d)
            self.corner_x(c, z, 1).wait_recv()
            self.corner_y(c, z, 1).wait_recv()
            if c not in self.direct:
                self.corner_z(c, z).start()
            self.on_core(c, 3, z, 0).start()

    def stage_pair(self, c):
        if c in self.direct:
            return
        for d in (1, 3):
            z = self.zof(d)
            self.corner_z(c, z).wait_recv()
            self.on_core(c, 3, z, 0).start()

    def stage_core(self, c):
        for kind in range(4):
            for z in range(4):
                self.on_core(c, kind, z, 1).wait_recv()

    def finish(self, c):
        for d in (1, 2, 3):
            self.to_z(c, self.zof(d)).wait_send()
        for z in range(4):
            self.on_x(c, z, 0).wait_send()
            self.on_y(c, z, 0).wait_send()
            for kind in range(4):
                self.on_core(c, kind, z, 0).wait_send()
        for d in self.corners(c):
            z = self.zof(d)
            self.corner_x(c, z, 0).wait_send()
            self.corner_y(c, z, 0).wait_send()
            if c not in self.direct:
                self.corner_z(c, z).wait_send()


def gather_sems(chunks):
    return [pltpu.SemaphoreType.DMA((chunks, 4))] * 12 + [pltpu.SemaphoreType.DMA((chunks, 16))] * 2


BF = jnp.bfloat16
F32 = jnp.float32
QB = 256
PLAN = ((0, 3, False, True), (0, 4, False, True), (0, 5, True, True), (1, 5, True, True))
HALO_PLAN = ((2, 2), (3, 1))
NEG = -1e30
VMEM_LIMIT = int(63.9 * 2**20)


def nn(a, b):
    return jnp.dot(a, b, preferred_element_type=F32)


def nt(a, b):
    return lax.dot_general(a, b, (((1,), (1,)), ((), ())), preferred_element_type=F32)


def tn(a, b):
    return lax.dot_general(a, b, (((0,), (0,)), ((), ())), preferred_element_type=F32)


def iota(shape, dim):
    return lax.broadcasted_iota(jnp.int32, shape, dim)


def block_at(flip, block):
    return pl.multiple_of(jnp.where(flip == 1, 3 - block, block) * QB, QB)


def rope(vectors, cosine, sine):
    lane = iota((1, 128), 1)
    first = lax.rem(lane, HEAD_DIM) < HEAD_DIM // 2
    out = []
    for c in range(vectors.shape[1] // 128):
        part = vectors[:, c * 128 : (c + 1) * 128]
        other = jnp.where(first, pltpu.roll(part, 96, 1), pltpu.roll(part, 32, 1))
        out.append(part * cosine + other * sine)
    return jnp.concatenate(out, axis=1)


def fill_tables(flip, seg_ref, freq_ref, cos_ref, sin_ref, fq_ref, fk_ref, bias_ref):
    lane = iota((1, 128), 1)
    seg_row = seg_ref[...].astype(F32)
    starts = [
        jnp.sum((seg_row < float(d)).astype(F32), axis=1, keepdims=True) for d in (1, 2, 3)
    ]
    sign = jnp.where(lax.rem(lane, HEAD_DIM) < HEAD_DIM // 2, -1.0, 1.0)
    for w in range(12):
        block, part = divmod(w, 2)
        base = jnp.where(flip == 1, 7 - block, block) * QB + part * 128
        row = seg_ref[:, pl.ds(pl.multiple_of(base, 128), 128)].astype(F32)
        seg = jnp.broadcast_to(row, (128, 128)).T
        start = jnp.where(
            seg >= 3.0,
            starts[2],
            jnp.where(seg >= 2.0, starts[1], jnp.where(seg >= 1.0, starts[0], 0.0)),
        )
        pos = (iota((128, 128), 0) + base).astype(F32) - start
        angle = pos * freq_ref[...]
        rows = pl.ds(w * 128, 128)
        cos_ref[rows, :] = jnp.cos(angle)
        sin_ref[rows, :] = jnp.sin(angle) * sign
        hit = seg == lane.astype(F32)
        fq_ref[rows, :] = jnp.where(hit, 1.0, 0.0).astype(BF)
        fk_ref[rows, :] = jnp.where(hit | (lane >= 4), 0.0, NEG).astype(BF)
    gap = iota((QB, QB), 0) - iota((QB, QB), 1)
    gap = jnp.where(flip == 1, -gap, gap)
    bias_ref[0] = jnp.where(gap >= 0, 0.0, NEG)
    bias_ref[1] = jnp.where(gap <= 0, 0.0, NEG)


def qkv_rows(p, rb, xw, wq, aqkv, bblk, cos_ref, sin_ref, dest, low_ref):
    rows = pl.ds(pl.multiple_of(rb * QB, QB), QB)
    x = xw[rows, :]
    if p == 0:
        low = nt(x, aqkv[...]).astype(BF)
        low_ref[rows, :] = low
    else:
        low = low_ref[rows, :]
    proj = nn(x, wq[p].reshape(D, D)) + nn(low, bblk[p])
    if p < 2:
        proj = rope(proj, cos_ref[rows, :], sin_ref[rows, :])
    value = proj.astype(BF)
    if p == 0:
        value = value * jnp.asarray(0.125, BF)
    dest[rb] = value


def attend_pair(
    qb, pair, step, q_ref, k_ref, v_ref, fq_ref, fk_ref, bias_ref, att_ref, linv_ref, mf_ref, p_hbm, stage, sem
):
    k0, n, tri_first, tri_last = PLAN[qb]
    rows = pl.ds(qb * QB, QB)
    kblocks = pl.ds(k0, n)
    krows = pl.ds(k0 * QB, n * QB)
    half = iota((1, 128), 1) >= HEAD_DIM
    lane = iota((1, 128), 1)
    slot = lax.rem(step, 2)

    def copy(s):
        return pltpu.make_async_copy(stage.at[pl.ds(s * 4, 4)], p_hbm.at[qb, pair], sem.at[s])

    @pl.when(pair >= 2)
    def _():
        copy(slot).wait()

    lanes = pl.ds(pl.multiple_of(pair * 128, 128), 128)
    q2 = q_ref[qb, :, lanes]
    fq = fq_ref[rows, :]
    keys = jnp.concatenate([k_ref[kblocks, :, lanes].reshape(n * QB, 128), fk_ref[krows, :]], axis=1)
    v2 = v_ref[kblocks, :, lanes].reshape(n * QB, 128)
    outs = []
    for h in range(2):
        mine = half if h == 1 else jnp.logical_not(half)
        qm = jnp.where(mine, q2, jnp.zeros_like(q2))
        s = nt(jnp.concatenate([qm, fq], axis=1), keys)
        parts = [s[:, t * QB : (t + 1) * QB] for t in range(n)]
        if tri_last:
            parts[n - 1] = parts[n - 1] + bias_ref[0]
        if tri_first:
            parts[0] = parts[0] + bias_ref[1]
        s = jnp.concatenate(parts, axis=1)
        m = jnp.max(s, axis=1, keepdims=True)
        p = jnp.exp(s - m).astype(BF)
        for g in range((n + 2) // 3):
            part = p[:, g * D : min(g * D + D, n * QB)]
            stage[slot * 4 + h * 2 + g, :, 0 : part.shape[1]] = part
        if qb >= 2:
            low = 4 + 3 * (2 * pair + h)
            mf_ref[rows, :] = jnp.where((lane >= low) & (lane < low + 3), -m, mf_ref[rows, :])
        outs.append(nn(p, jnp.where(mine, v2, jnp.ones_like(v2))))
    inv = 1.0 / pltpu.roll(jnp.where(half, outs[0], outs[1]), HEAD_DIM, 1)
    att_ref[rows, lanes] = (jnp.where(half, outs[1], outs[0]) * inv).astype(BF)
    linv_ref[rows, lanes] = inv
    copy(slot).start()


def drain_pairs(qb, p_hbm, stage, sem):
    for s in range(2):
        pltpu.make_async_copy(stage.at[pl.ds(s * 4, 4)], p_hbm.at[qb, 0], sem.at[s]).wait()


def norm_stats(r):
    centre = r - jnp.mean(r, axis=1, keepdims=True)
    rstd = lax.rsqrt(jnp.mean(centre * centre, axis=1, keepdims=True) + EPSILON)
    return centre * rstd, rstd


def norm_back(grad, xhat, rstd):
    return rstd * (
        grad
        - jnp.mean(grad, axis=1, keepdims=True)
        - xhat * jnp.mean(grad * xhat, axis=1, keepdims=True)
    )


def out_rows(rb, xw, att_ref, wo, ao, bo, gb, aff, xhat_ref, rstd_ref, act_ref, lowo_ref, lowf_ref):
    rows = pl.ds(pl.multiple_of(rb * QB, QB), QB)
    att = att_ref[rows, :]
    low = nt(att, ao[...]).astype(BF)
    lowo_ref[rows, :] = low
    branch = nn(att, wo[...].reshape(D, D)) + nn(low, bo[...])
    xhat, rstd = norm_stats(xw[rows, :].astype(F32) + branch)
    xhat_ref[rows, :] = xhat
    rstd_ref[rows, :] = jnp.broadcast_to(rstd, (QB, 128))
    act = (xhat * gb[0:1, :] + gb[1:2, :]).astype(BF)
    act_ref[rows, :] = act
    lowf_ref[rows, :] = nt(act, aff[...]).astype(BF)


def ffn_in_tile(n, rb, size, act_ref, lowf_ref, wi, wd, bg, bu, adn, big, lowd_ref, total_ref):
    start = pl.multiple_of(rb * size, size)
    rows = pl.ds(start, size)
    act = act_ref[rows, :]
    low = lowf_ref[rows, :]
    gate = nn(act, wi[n, 0].reshape(D, D)) + nn(low, bg[n])
    up = nn(act, wi[n, 1].reshape(D, D)) + nn(low, bu[n])
    inner = (gate * (1.0 / (1.0 + jnp.exp(-gate))) * up).astype(BF)
    blocks = size // QB
    here = n * 4 + rb * blocks
    big[pl.ds(here, blocks)] = gate.astype(BF).reshape(blocks, QB, D)
    big[pl.ds(here + 16, blocks)] = up.astype(BF).reshape(blocks, QB, D)
    lowd_ref[rows, 0:16] += nt(inner, adn[n])
    total_ref[rows, :] += nn(inner, wd[pl.ds(n * 8, 8)].reshape(D, D))


def ffn_out_rows(
    rb, flip, lowd_ref, bdn, xhat_ref, gb, cot, dtwo_ref, db2_ref, dlow_ref, mixed_ref, gbdn_ref
):
    start = pl.multiple_of(rb * QB, QB)
    rows = pl.ds(start, QB)
    low = lowd_ref[rows, 0:16].astype(BF)
    total = nn(low, bdn[...]) + dtwo_ref[rows, :]
    r = xhat_ref[rows, :] * gb[0:1, :] + gb[1:2, :] + total
    xhat, rstd = norm_stats(r)
    mixed_ref[pl.ds(block_at(flip, rb), QB), :] = (xhat * gb[2:3, :] + gb[3:4, :]).astype(BF)
    dtwo = norm_back(cot[rows, :].astype(F32) * gb[2:3, :], xhat, rstd)
    dtwo_ref[rows, :] = dtwo
    db2 = dtwo.astype(BF)
    db2_ref[rows, :] = db2
    dlow_ref[rows, :] = nt(db2, bdn[...]).astype(BF)
    gbdn_ref[...] += tn(low, db2)


def ffn_back_tile(
    n, start, size, db2_ref, dlow_ref, wd, wi, adn, bg, bu, big, lowf_ref, acc, dlf_ref, gadn_ref, gbf_ref
):
    rows = pl.ds(start, size)
    db2 = db2_ref[rows, :]
    dlow = dlow_ref[rows, :]
    dinner = nt(db2, wd[pl.ds(n * 8, 8)].reshape(D, D)) + nn(dlow, adn[n])
    blocks = size // QB
    here = n * 4 + lax.div(start, QB)
    gate = big[pl.ds(here, blocks)].reshape(size, D).astype(F32)
    up = big[pl.ds(here + 16, blocks)].reshape(size, D).astype(F32)
    sig = 1.0 / (1.0 + jnp.exp(-gate))
    silu = gate * sig
    inner = (silu * up).astype(BF)
    dg = (dinner * up * (sig + silu * (1.0 - sig))).astype(BF)
    du = (dinner * silu).astype(BF)
    acc[...] += nt(dg, wi[n, 0].reshape(D, D)) + nt(du, wi[n, 1].reshape(D, D))
    dlf_ref[...] += nt(dg, bg[n]) + nt(du, bu[n])
    gadn_ref[n] += tn(dlow, inner)
    low = lowf_ref[rows, :]
    gbf_ref[n] += jnp.where(iota((32, 1), 0) < 16, tn(low, dg), tn(low, du))


def hidden_back_rows(
    rb, off, acc, dlf_ref, aff, act_ref, dtwo_ref, xhat_ref, rstd_ref, gb, bo, ao, lowo_ref, att_ref,
    wo, linv_ref, h2, mf_ref, do_ref, hf_ref, gaff_ref, gbo_ref, gao_ref,
):
    start = pl.multiple_of(rb * QB, QB)
    rows = pl.ds(start, QB)
    local = pl.ds(pl.multiple_of(start - off, QB), QB)
    dlf = dlf_ref[local, :].astype(BF)
    dhid = dtwo_ref[rows, :] + acc[local, :] + nn(dlf, aff[...])
    gaff_ref[...] += tn(dlf, act_ref[rows, :])
    done = norm_back(dhid * gb[0:1, :], xhat_ref[rows, :], rstd_ref[rows, 0:1])
    dtwo_ref[rows, :] = done
    dbr = done.astype(BF)
    dlo = nt(dbr, bo[...]).astype(BF)
    att = att_ref[rows, :]
    gbo_ref[...] += tn(lowo_ref[rows, :], dbr)
    gao_ref[...] += tn(dlo, att)
    datt = (nt(dbr, wo[...].reshape(D, D)) + nn(dlo, ao[...])).astype(BF)
    do = (datt.astype(F32) * linv_ref[rows, :]).astype(BF)
    do_ref[rows, :] = do
    value = nn(do * att, h2[...]) + mf_ref[rows, :]
    lane = iota((1, 128), 1)
    role = jnp.where(lane < 40, lax.rem(lane + 2, 3), lax.rem(lane, 2))
    high = value.astype(BF)
    rest = value - high.astype(F32)
    mid = rest.astype(BF)
    last = (rest - mid.astype(F32)).astype(BF)
    hf_ref[rows, :] = jnp.where(role == 0, high, jnp.where(role == 1, mid, last))


def kf_kernel(
    x_hbm, cot_hbm, seg_ref, freq_ref, aqkv, bqkv, ao, bo, aff, bff, adn, bdn, gb, tag,
    wq_hbm, wo_hbm, wi_hbm, wd_hbm,
    q_hbm, k_hbm, v_hbm, p_hbm, mixed_hbm, do_hbm, hf_ref, lowq_hbm, done_hbm, cos_hbm, sin_hbm, fq_hbm, fk_hbm,
    ge_ref, wq_out,
    gao_ref, gaff_ref, gadn_ref, gbo_ref, gbdn_ref, gbf_ref,
    wq, wo, wi, wd, big, xw, att, linv, xhat, dtwo, act, db2, cos, sin, fq, fk, bias, mf,
    lowq, lowo, lowf, dlow, acc, dlf, bblk, bg, bu, h2, mixed_ref, do_ref, rsem, wsem, xsem, osem, psem, hs, hr, *sems,
):
    flip = lax.axis_index("seq")
    cot = db2
    rstd = cos
    lowd = sin
    loads = []
    for i in range(4):
        loads.append(
            pltpu.make_async_copy(
                x_hbm.at[pl.ds(block_at(flip, i), QB)], xw.at[pl.ds(i * QB, QB)], xsem.at[i]
            )
        )
        loads.append(
            pltpu.make_async_copy(
                cot_hbm.at[pl.ds(block_at(flip, i), QB)], cot.at[pl.ds(i * QB, QB)], xsem.at[4 + i]
            )
        )
    g = Gather(sems, direct=(0, 1, 2))

    def view(c, j, half):
        cut = 384 if c < 3 else 640
        lanes = slice(None) if half is None else pl.ds(0, cut) if half == 0 else pl.ds(cut, D - cut)
        if c < 3:
            return wq.at[c, j, :, lanes]
        if c == 3:
            return wo.at[j, :, lanes]
        if c < 6:
            return wd.at[j, pl.ds((c - 4) * 48, 48), lanes]
        return wi.at[c - 6, :, j, :, lanes]

    g.view = view
    weights = [
        pltpu.make_async_copy(a, b, wsem.at[i])
        for i, (a, b) in enumerate(
            [(wq_hbm, wq.at[:, g.me]), (wo_hbm, wo.at[g.me]), (wd_hbm, wd.at[g.me])]
            + [(wi_hbm.at[:, :, pl.ds(D * n, D)], wi.at[n, :, g.me]) for n in range(4)]
        )
    ]
    for copy in weights:
        copy.start()
    g.barrier()
    for copy in weights:
        copy.wait()
    for c in range(3):
        g.stage_own(c)
    for c in range(3, NCHUNK):
        g.send_z(c)
    halo = [
        pltpu.make_async_remote_copy(
            x_hbm.at[pl.ds(block_at(flip, 3 - i), QB)], xw.at[pl.ds(1024 + i * QB, QB)], hs.at[i], hr.at[i],
            device_id=g.devy, device_id_type=MESH,
        )
        for i in range(2)
    ]

    kinds = {
        "z": g.stage_z, "x": g.stage_xy, "c": g.stage_corner, "p": g.stage_pair, "k": g.stage_core, "s": g.send_xy,
    }

    def tick(*steps):
        for step in steps:
            kinds[step[0]](int(step[1]))

    for copy in loads:
        copy.start()
    fill_tables(flip, seg_ref, freq_ref, cos, sin, fq, fk, bias)
    rank = iota((48, 1), 0)
    for p in range(3):
        keep = (rank >= 16 * p) & (rank < 16 * p + 16)
        bblk[p] = jnp.where(keep, bqkv[...], jnp.zeros_like(bqkv[...]))
    rank = iota((32, 1), 0)
    for n in range(4):
        piece = bff[:, n * D : (n + 1) * D]
        bg[n] = jnp.where(rank < 16, piece, jnp.zeros_like(piece))
        bu[n] = jnp.where(rank >= 16, piece, jnp.zeros_like(piece))
    head = lax.div(iota((D, 128), 0), HEAD_DIM)
    spot = iota((D, 128), 1)
    h2[...] = jnp.where(lax.div(spot - 40, 2) == head, jnp.where(spot >= 40, -1.0, 0.0), 0.0).astype(BF)
    mf[...] = jnp.zeros_like(mf)
    dtwo[...] = jnp.zeros_like(dtwo)
    for ref in (gao_ref, gaff_ref, gadn_ref, gbo_ref, gbdn_ref, gbf_ref):
        ref[...] = jnp.zeros_like(ref)
    tick("z0", "z1", "z2", "s3", "x0", "x1", "x2")
    for copy in halo:
        copy.start()
    for copy in loads:
        copy.wait()
    tick("s4", "c0", "k0")
    q_ref, k_ref, v_ref = (big.at[pl.ds(i * 6, 6)] for i in range(3))
    stage = big.at[pl.ds(18, 8)]

    def qkv_page(p, first, last):
        def step(rb, _):
            qkv_rows(p, rb, xw, wq, aqkv, bblk, cos, sin, (q_ref, k_ref, v_ref)[p], lowq)
            return 0

        lax.fori_loop(first, last, step, 0)

    qkv_page(0, 0, 4)
    tick("c1", "k1", "z3", "s5")
    qkv_page(1, 0, 4)
    tick("c2", "k2", "x3", "z4")
    qkv_page(2, 0, 4)
    tick("c3", "x4", "z5", "s6")
    keep_wq = pltpu.make_async_copy(wq, wq_out, osem.at[9])
    keep_wq.start()
    for qb in range(4):

        def pair_step(pair, _, qb=qb):
            attend_pair(qb, pair, pair, q_ref, k_ref, v_ref, fq, fk, bias, att, linv, mf, p_hbm, stage, psem)
            return 0

        if qb < 2:
            lax.fori_loop(0, 6, pair_step, 0)
        else:
            lax.fori_loop(0, 3, pair_step, 0)
            tick(*(("c6", "x7", "s9") if qb == 2 else ("c7", "x8")))
            lax.fori_loop(3, 6, pair_step, 0)
        drain_pairs(qb, p_hbm, stage, psem)
        tick(
            *(
                ("p3", "c4", "x5", "z6", "s7"),
                ("k3", "p4", "c5", "x6", "z7", "s8"),
                ("k5", "p6", "z9"),
                ("k6", "p7", "x9"),
            )[qb]
        )
        if qb == 1:
            for copy in halo:
                copy.wait_recv()
            for p in range(3):
                qkv_page(p, 4, 6)
            tick("p5", "k4", "z8")
            saves = [
                pltpu.make_async_copy(a, b, osem.at[i])
                for i, (a, b) in enumerate(
                    ((q_ref, q_hbm), (k_ref, k_hbm), (v_ref, v_hbm), (lowq, lowq_hbm), (cos, cos_hbm), (sin, sin_hbm), (fq, fq_hbm), (fk, fk_hbm))
                )
            ]
            for copy in saves:
                copy.start()
    for copy in saves:
        copy.wait()
    lowd[...] = jnp.zeros_like(lowd)

    def out_step(rb, _):
        out_rows(rb, xw, att, wo, ao, bo, gb, aff, xhat, rstd, act, lowo, lowf)
        return 0

    lax.fori_loop(0, 4, out_step, 0)
    tick("c8")

    def in_step(i, _):
        ffn_in_tile(lax.div(i, 2), lax.rem(i, 2), 512, act, lowf, wi, wd, bg, bu, adn, big, lowd, dtwo)
        return 0

    lax.fori_loop(0, 2, in_step, 0)
    tick("k7", "p8", "c9")
    lax.fori_loop(2, 4, in_step, 0)
    tick("k8", "p9")
    lax.fori_loop(4, 6, in_step, 0)
    tick("k9")
    lax.fori_loop(6, 8, in_step, 0)

    def down_step(rb, _):
        ffn_out_rows(rb, flip, lowd, bdn, xhat, gb, cot, dtwo, db2, dlow, mixed_ref, gbdn_ref)
        return 0

    lax.fori_loop(0, 4, down_step, 0)
    outs = [pltpu.make_async_copy(mixed_ref, mixed_hbm, rsem.at[0])]
    outs[0].start()

    def row_copies(rb):
        rows = pl.ds(pl.multiple_of(rb * QB, QB), QB)
        return (
            pltpu.make_async_copy(do_ref.at[rows], do_hbm.at[rows], rsem.at[1 + rb]),
            pltpu.make_async_copy(dtwo.at[rows], done_hbm.at[rows], rsem.at[5 + rb]),
        )

    def back_step(half, _):
        off = pl.multiple_of(half * 512, 512)
        acc[...] = jnp.zeros_like(acc)
        dlf[...] = jnp.zeros_like(dlf)

        def tile(n, _):
            ffn_back_tile(
                n, off, 512, db2, dlow, wd, wi, adn, bg, bu, big, lowf, acc, dlf, gadn_ref, gbf_ref
            )
            return 0

        lax.fori_loop(0, 4, tile, 0)

        def rows(i, _):
            hidden_back_rows(
                half * 2 + i, off, acc, dlf, aff, act, dtwo, xhat, rstd, gb, bo, ao, lowo, att, wo, linv, h2, mf,
                do_ref, hf_ref, gaff_ref, gbo_ref, gao_ref,
            )
            for copy in row_copies(half * 2 + i):
                copy.start()
            return 0

        lax.fori_loop(0, 2, rows, 0)
        return 0

    lax.fori_loop(0, 2, back_step, 0)
    for rb in range(4):
        outs.extend(row_copies(rb))
    ge_ref[0:16] = gao_ref[...].astype(BF)
    ge_ref[16:48] = gaff_ref[...].astype(BF)
    ge_ref[48:64] = gbo_ref[...].astype(BF)
    ge_ref[64:80] = gbdn_ref[...].astype(BF)
    ge_ref[80:144] = gadn_ref[...].reshape(64, D).astype(BF)
    ge_ref[144:272] = gbf_ref[...].reshape(128, D).astype(BF)
    ge_ref[272:288] = tag[...]
    keep_wq.wait()
    for copy in outs:
        copy.wait()
    for copy in halo:
        copy.wait_send()
    for c in range(NCHUNK):
        g.finish(c)


def k3_kernel(
    x_hbm, q_hbm, k_hbm, v_hbm, p_hbm, do_hbm, hf_hbm, ge, lowq_hbm, done_hbm, cos_hbm, sin_hbm,
    fq_hbm, fk_hbm, aqkv, bqkv, wq_hbm,
    dx_ref, sum_e_ref, sum_l_ref,
    ga_ref, gbq_ref, dproj, eg, lg, ge_in, gl_out, gl_in,
    xw, q, k, v, do, hf, lowq, done, cos, sin, fq, fk, wq, stage, dq, dkT, dvT, bias, sem, psem, hs, hr, *sems,
):
    flip = lax.axis_index("seq")
    g = Gather(sems)
    table = (
        (q_hbm, q), (k_hbm, k), (v_hbm, v), (do_hbm, do.at[pl.ds(0, 1024)]), (hf_hbm, hf.at[pl.ds(0, 1024)]),
        (lowq_hbm, lowq), (done_hbm, done), (cos_hbm, cos), (sin_hbm, sin), (fq_hbm, fq), (fk_hbm, fk), (wq_hbm, wq),
    )
    loads = [pltpu.make_async_copy(a, b, sem.at[i]) for i, (a, b) in enumerate(table)]
    for i in range(4):
        loads.append(
            pltpu.make_async_copy(
                x_hbm.at[pl.ds(block_at(flip, i), QB)], xw.at[pl.ds(i * QB, QB)], sem.at[12 + i]
            )
        )
    for copy in loads:
        copy.start()

    def early(c, j, half):
        lanes = slice(None) if half is None else pl.ds(half * 384, 384)
        return eg.at[j, :, lanes]

    def late(c, j, half):
        lanes = slice(None) if half is None else pl.ds(half * 384, 384)
        return lg.at[j, :, lanes]

    g.barrier()
    halo = []
    for i, (src, dst) in enumerate(
        (
            (do_hbm.at[pl.ds(768, QB)], do.at[pl.ds(1024, QB)]),
            (do_hbm.at[pl.ds(512, QB)], do.at[pl.ds(1280, QB)]),
            (hf_hbm.at[pl.ds(768, QB)], hf.at[pl.ds(1024, QB)]),
            (hf_hbm.at[pl.ds(512, QB)], hf.at[pl.ds(1280, QB)]),
            (ge.at[pl.ds(pl.multiple_of((1 - flip) * 144, 16), 144)], ge_in),
            (gl_out.at[pl.ds(pl.multiple_of((1 - flip) * 48, 16), 48)], gl_in),
        )
    ):
        halo.append(
            pltpu.make_async_remote_copy(
                src, dst, hs.at[i], hr.at[i], device_id=g.devy, device_id_type=MESH
            )
        )
    for copy in (halo[4], halo[0], halo[1], halo[2], halo[3]):
        copy.start()
    dkT[...] = jnp.zeros_like(dkT)
    dvT[...] = jnp.zeros_like(dvT)
    ga_ref[...] = jnp.zeros_like(ga_ref)
    gbq_ref[...] = jnp.zeros_like(gbq_ref)
    gap = iota((QB, QB), 0) - iota((QB, QB), 1)
    gap = jnp.where(flip == 1, -gap, gap)
    bias[...] = jnp.where(gap <= 0, 0.0, NEG)
    half = iota((1, 128), 1) >= HEAD_DIM
    for copy in loads[:5]:
        copy.wait()

    def picks(pair, first, width):
        head = 2 * pair + lax.div(iota((128, 256), 1), 128)
        row = iota((128, 256), 0) - first - width * head
        return jnp.where((row >= 0) & (row < width), 1.0, 0.0).astype(BF)

    for qb in range(4):
        k0, n, _, _ = PLAN[qb]
        own = min(4 - k0, n)
        rows = pl.ds(qb * QB, QB)
        krows = pl.ds(k0 * QB, n * QB)

        def fetch(pair, s, qb=qb, n=n):
            return pltpu.make_async_copy(p_hbm.at[qb, pair], stage.at[s], psem.at[s])

        fetch(0, 0).start()

        def pair_step(pair, _, k0=k0, n=n, own=own, rows=rows, krows=krows, fetch=fetch):
            slot = lax.rem(pair, 2)
            fetch(pair, slot).wait()

            @pl.when(pair < 5)
            def _():
                fetch(pair + 1, 1 - slot).start()

            lanes = pl.ds(pl.multiple_of(pair * 128, 128), 128)
            do2 = do[rows, lanes]
            ndl = nn(hf[rows, :], picks(pair, 40, 2))
            k2 = k[krows, lanes]
            v2 = v[krows, lanes]
            qT = q[rows, lanes].T
            doT = do2.T
            dqs = []
            for h in range(2):
                mine = half if h == 1 else jnp.logical_not(half)
                p = stage[slot, 2 * h, :, 0 : min(D, n * QB)]
                if n > 3:
                    p = jnp.concatenate([p, stage[slot, 2 * h + 1, :, 0 : n * QB - D]], axis=1)
                dp = nt(jnp.where(mine, do2, jnp.zeros_like(do2)), v2)
                d = ndl[:, h * 128 : (h + 1) * 128]
                ds = (p.astype(F32) * (dp + jnp.concatenate([d] * (2 * n), axis=1))).astype(BF)
                dqs.append(nn(ds, k2))
                hr = pl.ds(pl.multiple_of(pair * 128 + h * 64, 64), 64)
                kc = pl.ds(k0 * QB, own * QB)
                dkT[hr, kc] += nn(qT[h * 64 : (h + 1) * 64], ds[:, 0 : own * QB])
                dvT[hr, kc] += nn(doT[h * 64 : (h + 1) * 64], p[:, 0 : own * QB])
            dq[rows, lanes] = jnp.where(half, dqs[1], dqs[0]) * 0.125
            return 0

        lax.fori_loop(0, 6, pair_step, 0)
        g.view = early
        if qb == 0:
            halo[4].wait_recv()
            mine = ge[pl.ds(pl.multiple_of(flip * 144, 16), 144)]
            total = mine.astype(F32) + ge_in[...].astype(F32)
            row = iota((144, 1), 0)
            eg[g.me] = jnp.where((row >= 128) & (flip == 1), mine.astype(F32), total).astype(BF)
            g.stage_own(0)
        elif qb == 1:
            g.stage_z(0)
        elif qb == 2:
            g.stage_xy(0)
        else:
            g.stage_corner(0)
            g.stage_pair(0)

    for copy in loads[5:]:
        copy.wait()
    for copy in halo[:4]:
        copy.wait_recv()
    for i, (k0, n) in enumerate(HALO_PLAN):
        rows = pl.ds(1024 + i * QB, QB)
        krows = pl.ds(k0 * QB, n * QB)

        def halo_step(pair, _, k0=k0, n=n, rows=rows, krows=krows):
            lanes = pl.ds(pl.multiple_of(pair * 128, 128), 128)
            do2 = do[rows, lanes]
            q2 = q[rows, lanes]
            feats = hf[rows, :]
            ndl = nn(feats, picks(pair, 40, 2))
            nm = nn(feats, picks(pair, 4, 3))
            keys = jnp.concatenate([k[krows, lanes], fk[krows, :]], axis=1)
            v2 = v[krows, lanes]
            qT = q2.T
            doT = do2.T
            for h in range(2):
                mine = half if h == 1 else jnp.logical_not(half)
                s = nt(jnp.concatenate([jnp.where(mine, q2, jnp.zeros_like(q2)), fq[rows, :]], axis=1), keys)
                parts = [s[:, t * QB : (t + 1) * QB] for t in range(n)]
                parts[0] = parts[0] + bias[...]
                s = jnp.concatenate(parts, axis=1)
                m = nm[:, h * 128 : (h + 1) * 128]
                p = jnp.exp(s + jnp.concatenate([m] * (2 * n), axis=1))
                dp = nt(jnp.where(mine, do2, jnp.zeros_like(do2)), v2)
                d = ndl[:, h * 128 : (h + 1) * 128]
                ds = (p * (dp + jnp.concatenate([d] * (2 * n), axis=1))).astype(BF)
                hr = pl.ds(pl.multiple_of(pair * 128 + h * 64, 64), 64)
                kc = pl.ds(k0 * QB, n * QB)
                dkT[hr, kc] += nn(qT[h * 64 : (h + 1) * 64], ds)
                dvT[hr, kc] += nn(doT[h * 64 : (h + 1) * 64], p.astype(BF))
            return 0

        lax.fori_loop(0, 6, halo_step, 0)

    g.stage_core(0)

    def weights_of(b, e):
        return eg[2 * b + 1, 128 + e : 129 + e, :].astype(F32)

    def sum_step(i, _):
        y = lax.div(i, 9)
        r = pl.multiple_of(lax.rem(i, 9) * 16, 16)
        totals = [jnp.zeros((16, D), F32) for _ in range(ADAPTERS)]
        for b in range(16):
            part = eg[2 * b + y, pl.ds(r, 16), :].astype(F32)
            for e in range(ADAPTERS):
                totals[e] += part * weights_of(b, e)
        for e in range(ADAPTERS):
            sum_e_ref[e, pl.ds(pl.multiple_of(i * 16, 16), 16), :] = totals[e]
        return 0

    lane = lax.div(iota((1, 48), 1), 16)
    rank = lax.div(iota((48, 1), 0), 16)

    def proj_step(rb, _):
        start = pl.multiple_of(rb * QB, QB)
        rows = pl.ds(start, QB)
        cosine = cos[rows, :]
        sine = -sin[rows, :]
        low = lowq[rows, :]
        dlow = jnp.zeros((QB, 48), F32)
        for p in range(3):
            if p == 0:
                d = rope(dq[rows, :], cosine, sine)
            else:
                src = (dkT, dvT)[p - 1]
                d = jnp.concatenate([src[pl.ds(c * 128, 128), rows].T for c in range(6)], axis=1)
                if p == 1:
                    d = rope(d, cosine, sine)
            d = d.astype(BF)
            dproj[p, rows, :] = d
            dlow += jnp.where(lane == p, nt(d, bqkv[...]), 0.0)
            gbq_ref[...] += jnp.where(rank == p, tn(low, d), 0.0)
        dlow = dlow.astype(BF)
        lowq[rows, :] = dlow
        ga_ref[...] += tn(dlow, xw[rows, :])
        return 0

    lax.fori_loop(0, 4, proj_step, 0)
    gl_out[0:48] = ga_ref[...].astype(BF)
    gl_out[48:96] = gbq_ref[...].astype(BF)
    halo[5].start()
    g.view = late

    def dx_rows(rb):
        rows = pl.ds(rb * QB, QB)
        total = done[rows, :] + nn(lowq[rows, :], aqkv[...])
        for p in range(3):
            total += nt(dproj[p, rows, :], wq[p].reshape(D, D))
        dx_ref[pl.ds(block_at(flip, rb), QB), :] = total.astype(BF)

    lax.fori_loop(0, 18, sum_step, 0)
    halo[5].wait_recv()
    lg[g.me] = (
        gl_out[pl.ds(pl.multiple_of(flip * 48, 16), 48)].astype(F32) + gl_in[...].astype(F32)
    ).astype(BF)
    g.stage_own(1)
    dx_rows(0)
    g.stage_z(1)
    dx_rows(1)
    g.stage_xy(1)
    dx_rows(2)
    g.stage_corner(1)
    dx_rows(3)
    g.stage_pair(1)
    g.stage_core(1)

    def late_step(i, _):
        y = lax.div(i, 3)
        r = pl.multiple_of(lax.rem(i, 3) * 16, 16)
        totals = [jnp.zeros((16, D), F32) for _ in range(ADAPTERS)]
        for b in range(16):
            part = lg[2 * b + y, pl.ds(r, 16), :].astype(F32)
            for e in range(ADAPTERS):
                totals[e] += part * weights_of(b, e)
        for e in range(ADAPTERS):
            sum_l_ref[e, pl.ds(pl.multiple_of(i * 16, 16), 16), :] = totals[e]
        return 0

    lax.fori_loop(0, 6, late_step, 0)
    for copy in halo:
        copy.wait_send()
    for c, view in enumerate((early, late)):
        g.view = view
        g.finish(c)


def sds(shape, dtype):
    return jax.ShapeDtypeStruct(shape, dtype)


ANY = functools.partial(pl.BlockSpec, memory_space=pl.ANY)
INV = functools.partial(pl.BlockSpec, memory_space=pltpu.VMEM)


def kf_call(*args):
    outs = [
        (ANY, (6, QB, D), BF), (ANY, (6, QB, D), BF), (ANY, (6, QB, D), BF), (ANY, (4, 6, 4, QB, D), BF),
        (ANY, (1024, D), BF), (ANY, (1024, D), BF), (INV, (1024, 128), BF),
        (ANY, (1536, 48), BF), (ANY, (1024, D), F32), (ANY, (1536, 128), F32), (ANY, (1536, 128), F32),
        (ANY, (1536, 128), BF), (ANY, (1536, 128), BF),
        (INV, (288, D), BF), (ANY, (3, 32, 24, D), BF),
    ]
    V = pltpu.VMEM
    scratch = [
        V((16, D), F32), V((32, D), F32), V((4, 16, D), F32), V((16, D), F32), V((16, D), F32), V((4, 32, D), F32),
        V((3, 32, 24, D), BF), V((32, 24, D), BF), V((4, 2, 32, 24, D), BF), V((32, 96, D), BF),
        V((32, QB, D), BF), V((1536, D), BF), V((1024, D), BF), V((1024, D), F32),
        V((1024, D), F32), V((1024, D), F32), V((1024, D), BF), V((1024, D), BF),
        V((1536, 128), F32), V((1536, 128), F32), V((1536, 128), BF), V((1536, 128), BF), V((2, QB, QB), F32),
        V((1024, 128), F32), V((1536, 48), BF), V((1024, 16), BF), V((1024, 32), BF),
        V((1024, 16), BF), V((512, D), F32), V((512, 32), F32), V((3, 48, D), BF),
        V((4, 32, D), BF), V((4, 32, D), BF), V((D, 128), BF), V((1024, D), BF), V((1024, D), BF),
        pltpu.SemaphoreType.DMA((9,)), pltpu.SemaphoreType.DMA((7,)), pltpu.SemaphoreType.DMA((8,)), pltpu.SemaphoreType.DMA((10,)),
        pltpu.SemaphoreType.DMA((2,)), pltpu.SemaphoreType.DMA((2,)), pltpu.SemaphoreType.DMA((2,)),
    ]
    scratch += gather_sems(NCHUNK)
    return pl.pallas_call(
        kf_kernel,
        out_shape=[sds(s, t) for _, s, t in outs],
        in_specs=[ANY()] * 2 + [INV()] * 12 + [ANY()] * 4,
        out_specs=[m() for m, _, _ in outs],
        scratch_shapes=scratch,
        compiler_params=pltpu.CompilerParams(
            vmem_limit_bytes=VMEM_LIMIT, collective_id=1, has_side_effects=True
        ),
    )(*args)


def k3_call(*args):
    V = pltpu.VMEM
    scratch = [
        V((48, D), F32), V((48, D), F32), V((3, 1024, D), BF), V((32, 144, D), BF), V((32, 48, D), BF),
        V((144, D), BF), V((96, D), BF), V((48, D), BF),
        V((1024, D), BF), V((1536, D), BF), V((1536, D), BF), V((1536, D), BF), V((1536, D), BF), V((1536, 128), BF),
        V((1536, 48), BF), V((1024, D), F32), V((1536, 128), F32), V((1536, 128), F32), V((1536, 128), BF),
        V((1536, 128), BF), V((3, 32, 24, D), BF), V((2, 4, QB, D), BF), V((1024, D), F32), V((D, 1024), F32),
        V((D, 1024), F32), V((QB, QB), F32), pltpu.SemaphoreType.DMA((16,)), pltpu.SemaphoreType.DMA((2,)),
        pltpu.SemaphoreType.DMA((6,)), pltpu.SemaphoreType.DMA((6,)),
    ]
    scratch += gather_sems(2)
    return pl.pallas_call(
        k3_kernel,
        out_shape=[sds((1024, D), BF), sds((4, 288, D), F32), sds((4, 96, D), F32)],
        in_specs=[ANY()] * 7 + [INV()] + [ANY()] * 6 + [INV()] * 2 + [ANY()],
        out_specs=[INV()] * 3,
        scratch_shapes=scratch,
        compiler_params=pltpu.CompilerParams(
            vmem_limit_bytes=VMEM_LIMIT, collective_id=2, has_side_effects=True
        ),
    )(*args)


def fast(
    tokens, cotangent, segments, adapter_index, qkv_weight, out_weight, ffn_in_weight, ffn_out_weight,
    norm_gain, norm_bias, adapt_in, adapt_down, adapt_out, adapt_ffn,
):
    x = tokens[0]
    e = adapter_index[0, 0]
    pick = lambda table: lax.dynamic_index_in_dim(table[0], e, 0, False)
    a_in = pick(adapt_in).transpose(0, 2, 1)
    aqkv, ao, aff = a_in[0:3].reshape(48, D), a_in[3], a_in[4:6].reshape(32, D)
    adn = pick(adapt_down).T.reshape(16, 4, D).transpose(1, 0, 2)
    b_out = pick(adapt_out)
    bqkv, bo, bdn = b_out[0:3].reshape(48, D), b_out[3], b_out[4]
    bff = pick(adapt_ffn).reshape(32, FF)
    gb = jnp.stack([norm_gain[0, 0], norm_bias[0, 0], norm_gain[0, 1], norm_bias[0, 1]])
    freq = jnp.power(ROPE_BASE, -2.0 * jnp.arange(HEAD_DIM // 2, dtype=F32) / HEAD_DIM)
    freq = jnp.tile(freq, 4)[None]
    tag = jnp.where(jnp.arange(16)[:, None] == e, 1.0, jnp.zeros((1, D))).astype(BF)
    q, k, v, p, mixed, do, hf, lowq, done, cos, sin, fq, fk, ge, wq = kf_call(
        x, cotangent[0], segments, freq, aqkv, bqkv, ao, bo, aff, bff, adn, bdn, gb, tag,
        qkv_weight[0], out_weight[0], ffn_in_weight[0], ffn_out_weight[0],
    )
    q, k, v = (a.reshape(1536, D) for a in (q, k, v))
    dx, se, sl = k3_call(x, q, k, v, p, do, hf, ge, lowq, done, cos, sin, fq, fk, aqkv, bqkv, wq)
    g_in = jnp.concatenate([sl[:, :48], se[:, :48]], axis=1).reshape(4, 6, 16, D)
    g_dn = se[:, 80:144].reshape(4, 4, 16, D).transpose(0, 2, 1, 3).reshape(4, 16, FF)
    g_out = jnp.concatenate([sl[:, 48:], se[:, 48:80]], axis=1).reshape(4, 5, 16, D)
    g_ff = se[:, 144:272].reshape(4, 4, 2, 16, D).transpose(0, 2, 3, 1, 4).reshape(4, 2, 16, FF)
    return (
        mixed[None], dx[None], g_in.transpose(0, 1, 3, 2)[None], g_dn.transpose(0, 2, 1)[None], g_out[None], g_ff[None],
    )


def solution(mesh):
    here = fast if dict(mesh.shape) == {"batch": 16, "seq": 2} else shards
    return jax.shard_map(
        here,
        mesh=mesh,
        in_specs=(
            P("batch", "seq", None),
            P("batch", "seq", None),
            P("batch", None),
            P("batch", None),
            P(None, None, ("batch", "seq"), None),
            P(None, ("batch", "seq"), None),
            P(None, None, ("batch", "seq"), None),
            P(None, ("batch", "seq"), None),
            P(),
            P(),
            P(),
            P(),
            P(),
            P(),
        ),
        out_specs=(P("batch", "seq", None), P("batch", "seq", None), P(), P(), P(), P()),
        check_vma=False,
    )
```

profile of v0, /device:TPU:1, one launch (start us, length us, event | category | flops | bytes accessed | tf_op | source)
XLA Modules:
  0.0 322.6 jit_solution(4462305115859984832)
XLA Ops:
  1.9 0.8 slice_bitcast_fusion.3
  3.3 0.7 broadcast_in_dim.36.tag
  4.0 1.4 dynamic-slice_bitcast_fusion.1
  5.4 1.5 constant_dynamic-slice_fusion
  6.9 0.9 constant_dynamic-slice_fusion.1
  7.8 0.6 copy.28
  8.4 0.9 dynamic-slice_bitcast_fusion
  10.6 0.6 slice.67
  11.2 1.6 constant_dynamic-slice_fusion.2
  12.8 174.2 %shard_map.181 = (bf16[6,256,768]{2,1,0:T(8,128)(2,1)}, bf16[6,256,768]{2,1,0:T(8,128)(2,1)}, bf16[6,256,768]{2,1,0:T(8,128)(2,1)}, bf16[4,6,4,256,768]{4,3,2,1,...) custom-call(bf16[1024,768]{1,0:T(8,128)(2,1)} %bitcast.67, ...), custom_call_target="tpu_custom_call" | custom-call | tf_op jit(solution)/shard_map/pallas_call | solution.py:1401
  187.0 119.6 %shard_map.182 = (bf16[1024,768]{1,0:T(8,128)(2,1)}, f32[4,288,768]{2,1,0:T(8,128)}, f32[4,96,768]{2,1,0:T(8,128)}) custom-call(bf16[1024,768]{1,0:T(8,128)(2,1)} %bitcast.68, bf16[1536,768]{1,0:T(8,128)(2,1)} %bitcast.70, bf16[1536,768]{1,0:T(8,128)(2,1)} %bitcast.71, bf16[1536,768]{1,0:T(8,128)(2,1)} %bitcast.72, ...), custom_call_target="tpu_custom_call" | custom-call | tf_op jit(solution)/shard_map/pallas_call | solution.py:1425
  306.6 1.0 slice.65
  307.7 1.1 slice.62
  308.8 1.2 slice.63
  310.0 1.5 slice.66
  311.5 1.0 copy.24
  312.5 2.0 broadcast_in_dim_reshape.7
  314.5 0.9 copy.26
  316.1 1.0 pad_maximum_fusion.1
  317.2 1.1 pad_maximum_fusion
  318.3 0.7 copy-done
  319.0 1.1 copy.32
  320.1 0.8 copy-done.1
  321.0 1.1 copy.33
  (12 shorter events, 3.2 us)
Async XLA Ops:
  314.5 1.6 copy-start.2
  317.2 1.8 copy-start
  319.0 2.0 copy-start.1
where the time goes:
time: 328 us; the launch traced here: 323 us
  Pallas kernels  294 us (90%)
  local copies, waits for them, and re-layouts  24.2 us (7%)
    pallas_call x1, Pallas kernels, kf_call(): pl.pallas_call(kf_kernel, out_shape=[sds(s, t) for _, s, t in outs], in_s...  174 us
    pallas_call x1, Pallas kernels, k3_call(): pl.pallas_call(k3_kernel, out_shape=[sds((1024, D), BF), sds((4, 288, D),...  120 us

commit v1 on v0

--- a/solution.py
+++ b/solution.py
@@ -3,6 +3,7 @@
 
 import jax
 import jax.numpy as jnp
+import numpy as np
 from jax import lax
 from jax.experimental import pallas as pl
 from jax.experimental.pallas import tpu as pltpu
@@ -471,73 +472,81 @@
 
 MESH = pl.DeviceIdType.MESH
 NCHUNK = 10
+ALL = slice(None)
 
 
 class Gather:
-    def __init__(self, sems, direct=()):
+    def __init__(self, sems, direct=(), diagonal=()):
         self.direct = direct
+        self.diagonal = diagonal
         (
             self.zs, self.zr, self.xs, self.xr, self.ys, self.yr, self.ds, self.dr, self.es, self.er, self.fs, self.fr,
             self.cs, self.cr,
         ) = sems
         b = lax.axis_index("batch")
+        self.b = b
         self.s = lax.axis_index("seq")
         self.core = lax.rem(b, 2)
         self.x = lax.rem(lax.div(b, 2), 2)
         self.z = lax.div(b, 4)
+        self.za = lax.div(self.z, 2)
+        self.zb = lax.rem(self.z, 2)
         self.devx = (b + 2 - 4 * self.x, self.s)
         self.devy = (b, 1 - self.s)
+        self.devd = (b + 2 - 4 * self.x, 1 - self.s)
         self.devc = (b + 1 - 2 * self.core, self.s)
-        self.pair = self.z + 1 - 2 * lax.rem(self.z, 2)
-        self.me = self.owner(self.z, 0, 0, 0)
-
-    def owner(self, z, dx, dy, dc):
+        self.devp = (b + 4 - 8 * self.zb, self.s)
+
+    def column(self, dx, dy, dc):
         x = 1 - self.x if dx else self.x
         y = 1 - self.s if dy else self.s
         c = 1 - self.core if dc else self.core
-        return (z * 4 + x * 2 + c) * 2 + y
+        return (x * 2 + c) * 2 + y
 
     def devz(self, z):
         return (z * 4 + self.x * 2 + self.core, self.s)
 
-    def zof(self, d):
-        return lax.rem(self.z + d, 4)
-
-    def copy(self, c, j, half, dev, send, recv):
-        v = self.view(c, j, half)
+    def copy(self, c, za, zb, k, half, dev, send, recv):
+        v = self.view(c, za, zb, k, half)
         return pltpu.make_async_remote_copy(v, v, send, recv, device_id=dev, device_id_type=MESH)
 
     def to_z(self, c, z):
-        return self.copy(c, self.me, None, self.devz(z), self.zs.at[c, z], self.zr.at[c, self.z])
+        return self.copy(
+            c, self.za, self.zb, self.column(0, 0, 0), None, self.devz(z), self.zs.at[c, z], self.zr.at[c, self.z]
+        )
 
     def from_z(self, c, z):
-        return self.copy(c, self.owner(z, 0, 0, 0), None, self.devz(z), self.zs.at[c, z], self.zr.at[c, z])
-
-    def on_x(self, c, z, arriving):
-        return self.copy(c, self.owner(z, arriving, 0, 0), None, self.devx, self.xs.at[c, z], self.xr.at[c, z])
-
-    def on_y(self, c, z, arriving):
-        return self.copy(c, self.owner(z, 0, arriving, 0), None, self.devy, self.ys.at[c, z], self.yr.at[c, z])
-
-    def corner_x(self, c, z, arriving):
-        return self.copy(c, self.owner(z, arriving, 1, 0), 0, self.devx, self.ds.at[c, z], self.dr.at[c, z])
-
-    def corner_y(self, c, z, arriving):
-        return self.copy(c, self.owner(z, 1, arriving, 0), 1, self.devy, self.es.at[c, z], self.er.at[c, z])
-
-    def corner_z(self, c, z):
-        return self.copy(c, self.owner(z, 1, 1, 0), None, self.devz(self.pair), self.fs.at[c, z], self.fr.at[c, z])
-
-    def on_core(self, c, kind, z, arriving):
-        j = self.owner(z, kind & 1, kind >> 1, arriving)
-        k = kind * 4 + z
-        return self.copy(c, j, None, self.devc, self.cs.at[c, k], self.cr.at[c, k])
-
-    def barrier(self):
-        bar = pltpu.get_barrier_semaphore()
-        for dev in (self.devx, self.devy, self.devc, self.devz(self.zof(1)), self.devz(self.zof(2)), self.devz(self.zof(3))):
-            pl.semaphore_signal(bar, inc=1, device_id=dev, device_id_type=MESH)
-        pl.semaphore_wait(bar, 6)
+        return self.copy(
+            c, lax.div(z, 2), lax.rem(z, 2), self.column(0, 0, 0), None, self.devz(z), self.zs.at[c, z], self.zr.at[c, z]
+        )
+
+    def on_x(self, c, arriving):
+        return self.copy(c, ALL, ALL, self.column(arriving, 0, 0), None, self.devx, self.xs.at[c], self.xr.at[c])
+
+    def on_y(self, c, arriving):
+        return self.copy(c, ALL, ALL, self.column(0, arriving, 0), None, self.devy, self.ys.at[c], self.yr.at[c])
+
+    def on_diagonal(self, c, arriving):
+        return self.copy(c, ALL, ALL, self.column(arriving, arriving, 0), None, self.devd, self.ds.at[c], self.dr.at[c])
+
+    def parity(self, c):
+        return ALL if c in self.direct else self.zb
+
+    def corner_x(self, c, arriving):
+        k = self.column(arriving, 1, 0)
+        return self.copy(c, ALL, self.parity(c), k, 0, self.devx, self.ds.at[c], self.dr.at[c])
+
+    def corner_y(self, c, arriving):
+        k = self.column(1, arriving, 0)
+        return self.copy(c, ALL, self.parity(c), k, 1, self.devy, self.es.at[c], self.er.at[c])
+
+    def corner_z(self, c, arriving):
+        zb = 1 - self.zb if arriving else self.zb
+        return self.copy(c, ALL, zb, self.column(1, 1, 0), None, self.devp, self.fs.at[c], self.fr.at[c])
+
+    def on_core(self, c, kind, arriving):
+        k = self.column(kind & 1, kind >> 1, arriving)
+        return self.copy(c, ALL, ALL, k, None, self.devc, self.cs.at[c, kind], self.cr.at[c, kind])
 
     def others(self):
         z = self.z
@@ -546,81 +555,77 @@
         third = jnp.where(z <= 1, 3, 0)
         return first, second, third
 
-    def corners(self, c):
-        return (0, 1, 2, 3) if c in self.direct else (0, 2)
+    def partners(self):
+        return [self.devx, self.devy, self.devc] + [self.devz(z) for z in self.others()]
+
+    def barrier(self, devices):
+        bar = pltpu.get_barrier_semaphore()
+        for dev in devices:
+            pl.semaphore_signal(bar, inc=1, device_id=dev, device_id_type=MESH)
+        pl.semaphore_wait(bar, len(devices))
 
     def send_z(self, c):
         for z in self.others():
             self.to_z(c, z).start()
 
-    def send_xy(self, c):
-        self.on_x(c, self.z, 0).start()
-        self.on_y(c, self.z, 0).start()
-        self.on_core(c, 0, self.z, 0).start()
-
-    def stage_own(self, c):
-        self.send_z(c)
-        self.send_xy(c)
-
     def stage_z(self, c):
         for z in self.others():
             self.from_z(c, z).wait_recv()
-            self.on_x(c, z, 0).start()
-            self.on_y(c, z, 0).start()
-            self.on_core(c, 0, z, 0).start()
+        self.on_x(c, 0).start()
+        self.on_y(c, 0).start()
+        if c in self.diagonal:
+            self.on_diagonal(c, 0).start()
+        self.on_core(c, 0, 0).start()
 
     def stage_xy(self, c):
-        for d in (0, 2, 1, 3):
-            z = self.zof(d)
-            self.on_x(c, z, 1).wait_recv()
-            if d in self.corners(c):
-                self.corner_y(c, z, 0).start()
-            self.on_core(c, 1, z, 0).start()
-            self.on_y(c, z, 1).wait_recv()
-            if d in self.corners(c):
-                self.corner_x(c, z, 0).start()
-            self.on_core(c, 2, z, 0).start()
+        self.on_x(c, 1).wait_recv()
+        if c not in self.diagonal:
+            self.corner_y(c, 0).start()
+        self.on_core(c, 1, 0).start()
+        self.on_y(c, 1).wait_recv()
+        if c not in self.diagonal:
+            self.corner_x(c, 0).start()
+        self.on_core(c, 2, 0).start()
+        if c in self.diagonal:
+            self.on_diagonal(c, 1).wait_recv()
+            self.on_core(c, 3, 0).start()
 
     def stage_corner(self, c):
-        for d in self.corners(c):
-            z = self.zof(d)
-            self.corner_x(c, z, 1).wait_recv()
-            self.corner_y(c, z, 1).wait_recv()
-            if c not in self.direct:
-                self.corner_z(c, z).start()
-            self.on_core(c, 3, z, 0).start()
+        self.corner_x(c, 1).wait_recv()
+        self.corner_y(c, 1).wait_recv()
+        if c in self.direct:
+            self.on_core(c, 3, 0).start()
+        else:
+            self.corner_z(c, 0).start()
 
     def stage_pair(self, c):
-        if c in self.direct:
-            return
-        for d in (1, 3):
-            z = self.zof(d)
-            self.corner_z(c, z).wait_recv()
-            self.on_core(c, 3, z, 0).start()
+        self.corner_z(c, 1).wait_recv()
+        self.on_core(c, 3, 0).start()
 
     def stage_core(self, c):
         for kind in range(4):
-            for z in range(4):
-                self.on_core(c, kind, z, 1).wait_recv()
+            self.on_core(c, kind, 1).wait_recv()
 
     def finish(self, c):
-        for d in (1, 2, 3):
-            self.to_z(c, self.zof(d)).wait_send()
-        for z in range(4):
-            self.on_x(c, z, 0).wait_send()
-            self.on_y(c, z, 0).wait_send()
-            for kind in range(4):
-                self.on_core(c, kind, z, 0).wait_send()
-        for d in self.corners(c):
-            z = self.zof(d)
-            self.corner_x(c, z, 0).wait_send()
-            self.corner_y(c, z, 0).wait_send()
+        for z in self.others():
+            self.to_z(c, z).wait_send()
+        self.on_x(c, 0).wait_send()
+        self.on_y(c, 0).wait_send()
+        for kind in range(4):
+            self.on_core(c, kind, 0).wait_send()
+        if c in self.diagonal:
+            self.on_diagonal(c, 0).wait_send()
+        else:
+            self.corner_x(c, 0).wait_send()
+            self.corner_y(c, 0).wait_send()
             if c not in self.direct:
-                self.corner_z(c, z).wait_send()
+                self.corner_z(c, 0).wait_send()
 
 
 def gather_sems(chunks):
-    return [pltpu.SemaphoreType.DMA((chunks, 4))] * 12 + [pltpu.SemaphoreType.DMA((chunks, 16))] * 2
+    one = pltpu.SemaphoreType.DMA((chunks,))
+    four = pltpu.SemaphoreType.DMA((chunks, 4))
+    return [four] * 2 + [one] * 10 + [four] * 2
 
 
 BF = jnp.bfloat16
@@ -695,7 +700,7 @@
 
 
 def qkv_rows(p, rb, xw, wq, aqkv, bblk, cos_ref, sin_ref, dest, low_ref):
-    rows = pl.ds(pl.multiple_of(rb * QB, QB), QB)
+    rows = pl.ds(pl.multiple_of(rb * 512, 512), 512)
     x = xw[rows, :]
     if p == 0:
         low = nt(x, aqkv[...]).astype(BF)
@@ -708,7 +713,16 @@
     value = proj.astype(BF)
     if p == 0:
         value = value * jnp.asarray(0.125, BF)
-    dest[rb] = value
+    dest[pl.ds(rb * 2, 2)] = value.reshape(2, QB, D)
+
+
+def prob_copies(n, src, dst, sem, s):
+    full = (2 * n + 2) // 3
+    cuts = ((0, 2), (2, full)) if full > 2 else ((0, 1), (1, 2))
+    return [
+        pltpu.make_async_copy(src.at[pl.ds(a, b - a)], dst.at[pl.ds(a, b - a)], sem.at[2 * s + i])
+        for i, (a, b) in enumerate(cuts)
+    ]
 
 
 def attend_pair(
@@ -723,11 +737,12 @@
     slot = lax.rem(step, 2)
 
     def copy(s):
-        return pltpu.make_async_copy(stage.at[pl.ds(s * 4, 4)], p_hbm.at[qb, pair], sem.at[s])
+        return prob_copies(n, stage.at[pl.ds(s * 4, 4)], p_hbm.at[qb, pair], sem, s)
 
     @pl.when(pair >= 2)
     def _():
-        copy(slot).wait()
+        for one in copy(slot):
+            one.wait()
 
     lanes = pl.ds(pl.multiple_of(pair * 128, 128), 128)
     q2 = q_ref[qb, :, lanes]
@@ -747,9 +762,9 @@
         s = jnp.concatenate(parts, axis=1)
         m = jnp.max(s, axis=1, keepdims=True)
         p = jnp.exp(s - m).astype(BF)
-        for g in range((n + 2) // 3):
-            part = p[:, g * D : min(g * D + D, n * QB)]
-            stage[slot * 4 + h * 2 + g, :, 0 : part.shape[1]] = part
+        for t in range(n):
+            block, lane0 = divmod(h * n + t, 3)
+            stage[slot * 4 + block, :, lane0 * QB : lane0 * QB + QB] = p[:, t * QB : (t + 1) * QB]
         if qb >= 2:
             low = 4 + 3 * (2 * pair + h)
             mf_ref[rows, :] = jnp.where((lane >= low) & (lane < low + 3), -m, mf_ref[rows, :])
@@ -757,12 +772,14 @@
     inv = 1.0 / pltpu.roll(jnp.where(half, outs[0], outs[1]), HEAD_DIM, 1)
     att_ref[rows, lanes] = (jnp.where(half, outs[1], outs[0]) * inv).astype(BF)
     linv_ref[rows, lanes] = inv
-    copy(slot).start()
+    for one in copy(slot):
+        one.start()
 
 
 def drain_pairs(qb, p_hbm, stage, sem):
     for s in range(2):
-        pltpu.make_async_copy(stage.at[pl.ds(s * 4, 4)], p_hbm.at[qb, 0], sem.at[s]).wait()
+        for one in prob_copies(PLAN[qb][1], stage.at[pl.ds(s * 4, 4)], p_hbm.at[qb, 0], sem, s):
+            one.wait()
 
 
 def norm_stats(r):
@@ -798,15 +815,19 @@
     rows = pl.ds(start, size)
     act = act_ref[rows, :]
     low = lowf_ref[rows, :]
-    gate = nn(act, wi[n, 0].reshape(D, D)) + nn(low, bg[n])
-    up = nn(act, wi[n, 1].reshape(D, D)) + nn(low, bu[n])
-    inner = (gate * (1.0 / (1.0 + jnp.exp(-gate))) * up).astype(BF)
     blocks = size // QB
     here = n * 4 + rb * blocks
-    big[pl.ds(here, blocks)] = gate.astype(BF).reshape(blocks, QB, D)
-    big[pl.ds(here + 16, blocks)] = up.astype(BF).reshape(blocks, QB, D)
+    parts = []
+    for c in range(3):
+        lanes = slice(c * 256, c * 256 + 256)
+        gate = nn(act, wi[n, 0, :, :, :, :, lanes].reshape(D, 256)) + nn(low, bg[n, :, lanes])
+        up = nn(act, wi[n, 1, :, :, :, :, lanes].reshape(D, 256)) + nn(low, bu[n, :, lanes])
+        parts.append((gate * (1.0 / (1.0 + jnp.exp(-gate))) * up).astype(BF))
+        big[pl.ds(here, blocks), :, lanes] = gate.astype(BF).reshape(blocks, QB, 256)
+        big[pl.ds(here + 16, blocks), :, lanes] = up.astype(BF).reshape(blocks, QB, 256)
+    inner = jnp.concatenate(parts, axis=1)
     lowd_ref[rows, 0:16] += nt(inner, adn[n])
-    total_ref[rows, :] += nn(inner, wd[pl.ds(n * 8, 8)].reshape(D, D))
+    total_ref[rows, :] += nn(inner, wd[lax.div(n, 2), lax.rem(n, 2)].reshape(D, D))
 
 
 def ffn_out_rows(
@@ -833,16 +854,21 @@
     rows = pl.ds(start, size)
     db2 = db2_ref[rows, :]
     dlow = dlow_ref[rows, :]
-    dinner = nt(db2, wd[pl.ds(n * 8, 8)].reshape(D, D)) + nn(dlow, adn[n])
     blocks = size // QB
     here = n * 4 + lax.div(start, QB)
-    gate = big[pl.ds(here, blocks)].reshape(size, D).astype(F32)
-    up = big[pl.ds(here + 16, blocks)].reshape(size, D).astype(F32)
-    sig = 1.0 / (1.0 + jnp.exp(-gate))
-    silu = gate * sig
-    inner = (silu * up).astype(BF)
-    dg = (dinner * up * (sig + silu * (1.0 - sig))).astype(BF)
-    du = (dinner * silu).astype(BF)
+    down = wd[lax.div(n, 2), lax.rem(n, 2)].reshape(D, D)
+    dgs, dus, inners = [], [], []
+    for c in range(3):
+        lanes = slice(c * 256, c * 256 + 256)
+        dinner = nt(db2, down[lanes]) + nn(dlow, adn[n, :, lanes])
+        gate = big[pl.ds(here, blocks), :, lanes].reshape(size, 256).astype(F32)
+        up = big[pl.ds(here + 16, blocks), :, lanes].reshape(size, 256).astype(F32)
+        sig = 1.0 / (1.0 + jnp.exp(-gate))
+        silu = gate * sig
+        inners.append((silu * up).astype(BF))
+        dgs.append((dinner * up * (sig + silu * (1.0 - sig))).astype(BF))
+        dus.append((dinner * silu).astype(BF))
+    dg, du, inner = (jnp.concatenate(v, axis=1) for v in (dgs, dus, inners))
     acc[...] += nt(dg, wi[n, 0].reshape(D, D)) + nt(du, wi[n, 1].reshape(D, D))
     dlf_ref[...] += nt(dg, bg[n]) + nt(du, bu[n])
     gadn_ref[n] += tn(dlow, inner)
@@ -881,13 +907,14 @@
 
 
 def kf_kernel(
-    x_hbm, cot_hbm, seg_ref, freq_ref, aqkv, bqkv, ao, bo, aff, bff, adn, bdn, gb, tag,
+    x_hbm, cot_hbm, seg_ref, freq_ref, pick_ref, gain_ref, shift_ref, tin_hbm, tdn_hbm, tout_hbm, tff_hbm,
     wq_hbm, wo_hbm, wi_hbm, wd_hbm,
     q_hbm, k_hbm, v_hbm, p_hbm, mixed_hbm, do_hbm, hf_ref, lowq_hbm, done_hbm, cos_hbm, sin_hbm, fq_hbm, fk_hbm,
-    ge_ref, wq_out,
-    gao_ref, gaff_ref, gadn_ref, gbo_ref, gbdn_ref, gbf_ref,
+    ge_ref, gao_ref, tag_ref, aqkv, bqkv, wq_out,
+    ao, bo, aff, adn, bdn, gb,
+    gaff_ref, gadn_ref, gbo_ref, gbdn_ref, gbf_ref,
     wq, wo, wi, wd, big, xw, att, linv, xhat, dtwo, act, db2, cos, sin, fq, fk, bias, mf,
-    lowq, lowo, lowf, dlow, acc, dlf, bblk, bg, bu, h2, mixed_ref, do_ref, rsem, wsem, xsem, osem, psem, hs, hr, *sems,
+    lowq, lowo, lowf, dlow, acc, dlf, bblk, bg, bu, h2, mixed_ref, do_ref, rsem, tsem, wsem, xsem, osem, psem, hs, hr, *sems,
 ):
     flip = lax.axis_index("seq")
     cot = db2
@@ -905,62 +932,89 @@
                 cot_hbm.at[pl.ds(block_at(flip, i), QB)], cot.at[pl.ds(i * QB, QB)], xsem.at[4 + i]
             )
         )
+    tables = [
+        (tin_hbm, big.at[pl.ds(0, ADAPTERS), pl.ds(0, 96)]),
+        (tout_hbm, big.at[pl.ds(4, ADAPTERS), pl.ds(0, 80)]),
+    ]
+    for n in range(4):
+        lanes = pl.ds(n * D, D)
+        tables.append((tdn_hbm.at[:, :, lanes], big.at[pl.ds(8, ADAPTERS), pl.ds(16 * n, 16)]))
+        tables.append((tff_hbm.at[:, :, lanes], big.at[pl.ds(12, ADAPTERS), pl.ds(32 * n, 32)]))
+    tables = [pltpu.make_async_copy(a, b, tsem.at[i]) for i, (a, b) in enumerate(tables)]
     g = Gather(sems, direct=(0, 1, 2))
 
-    def view(c, j, half):
+    def view(c, za, zb, k, half):
         cut = 384 if c < 3 else 640
-        lanes = slice(None) if half is None else pl.ds(0, cut) if half == 0 else pl.ds(cut, D - cut)
+        lanes = ALL if half is None else pl.ds(0, cut) if half == 0 else pl.ds(cut, D - cut)
         if c < 3:
-            return wq.at[c, j, :, lanes]
+            return wq.at[c, za, zb, k, :, lanes]
         if c == 3:
-            return wo.at[j, :, lanes]
+            return wo.at[za, zb, k, :, lanes]
         if c < 6:
-            return wd.at[j, pl.ds((c - 4) * 48, 48), lanes]
-        return wi.at[c - 6, :, j, :, lanes]
+            return wd.at[za, zb, k, pl.ds((c - 4) * 48, 48), lanes]
+        return wi.at[c - 6, :, za, zb, k, :, lanes]
 
     g.view = view
+    here = g.column(0, 0, 0)
     weights = [
         pltpu.make_async_copy(a, b, wsem.at[i])
         for i, (a, b) in enumerate(
-            [(wq_hbm, wq.at[:, g.me]), (wo_hbm, wo.at[g.me]), (wd_hbm, wd.at[g.me])]
-            + [(wi_hbm.at[:, :, pl.ds(D * n, D)], wi.at[n, :, g.me]) for n in range(4)]
+            [(wq_hbm, wq.at[:, g.za, g.zb, here]), (wo_hbm, wo.at[g.za, g.zb, here]), (wd_hbm, wd.at[g.za, g.zb, here])]
+            + [(wi_hbm.at[:, :, pl.ds(D * n, D)], wi.at[n, :, g.za, g.zb, here]) for n in range(4)]
         )
     ]
     for copy in weights:
         copy.start()
-    g.barrier()
+    g.barrier(g.partners())
     for copy in weights:
         copy.wait()
-    for c in range(3):
-        g.stage_own(c)
-    for c in range(3, NCHUNK):
+    for c in range(NCHUNK):
         g.send_z(c)
     halo = [
         pltpu.make_async_remote_copy(
-            x_hbm.at[pl.ds(block_at(flip, 3 - i), QB)], xw.at[pl.ds(1024 + i * QB, QB)], hs.at[i], hr.at[i],
-            device_id=g.devy, device_id_type=MESH,
-        )
-        for i in range(2)
+            x_hbm.at[pl.ds(block_at(flip, 3 - i // 2) + i % 2 * 128, 128)], xw.at[pl.ds(1024 + i * 128, 128)],
+            hs.at[i], hr.at[i], device_id=g.devy, device_id_type=MESH,
+        )
+        for i in range(4)
     ]
 
     kinds = {
-        "z": g.stage_z, "x": g.stage_xy, "c": g.stage_corner, "p": g.stage_pair, "k": g.stage_core, "s": g.send_xy,
+        "z": g.stage_z, "x": g.stage_xy, "c": g.stage_corner, "p": g.stage_pair, "k": g.stage_core,
     }
 
     def tick(*steps):
         for step in steps:
-            kinds[step[0]](int(step[1]))
-
-    for copy in loads:
+            if step[0] == "h":
+                halo[int(step[1])].start()
+            else:
+                kinds[step[0]](int(step[1]))
+
+    tick("h0")
+    for copy in loads + tables:
         copy.start()
     fill_tables(flip, seg_ref, freq_ref, cos, sin, fq, fk, bias)
+    for copy in tables:
+        copy.wait()
+    e = pick_ref[0, 0]
+    aqkv[...] = big[e, 0:48, :]
+    ao[...] = big[e, 48:64, :]
+    aff[...] = big[e, 64:96, :]
+    bqkv[...] = big[4 + e, 0:48, :]
+    bo[...] = big[4 + e, 48:64, :]
+    bdn[...] = big[4 + e, 64:80, :]
+    for n in range(4):
+        adn[n] = big[8 + e, 16 * n : 16 * n + 16, :]
+    tag_ref[...] = jnp.where(iota((16, 128), 0) == e, 1.0, 0.0).astype(BF)
+    for i in range(2):
+        gb[2 * i : 2 * i + 1, :] = gain_ref[i : i + 1, :]
+        gb[2 * i + 1 : 2 * i + 2, :] = shift_ref[i : i + 1, :]
     rank = iota((48, 1), 0)
     for p in range(3):
         keep = (rank >= 16 * p) & (rank < 16 * p + 16)
         bblk[p] = jnp.where(keep, bqkv[...], jnp.zeros_like(bqkv[...]))
     rank = iota((32, 1), 0)
     for n in range(4):
-        piece = bff[:, n * D : (n + 1) * D]
+        piece = big[12 + e, 32 * n : 32 * n + 32, :]
         bg[n] = jnp.where(rank < 16, piece, jnp.zeros_like(piece))
         bu[n] = jnp.where(rank >= 16, piece, jnp.zeros_like(piece))
     head = lax.div(iota((D, 128), 0), HEAD_DIM)
@@ -970,12 +1024,10 @@
     dtwo[...] = jnp.zeros_like(dtwo)
     for ref in (gao_ref, gaff_ref, gadn_ref, gbo_ref, gbdn_ref, gbf_ref):
         ref[...] = jnp.zeros_like(ref)
-    tick("z0", "z1", "z2", "s3", "x0", "x1", "x2")
-    for copy in halo:
-        copy.start()
+    tick("z0", "z1", "x0", "z2", "x1", "h1", "z3")
     for copy in loads:
         copy.wait()
-    tick("s4", "c0", "k0")
+    tick("c0", "k0")
     q_ref, k_ref, v_ref = (big.at[pl.ds(i * 6, 6)] for i in range(3))
     stage = big.at[pl.ds(18, 8)]
 
@@ -986,12 +1038,12 @@
 
         lax.fori_loop(first, last, step, 0)
 
-    qkv_page(0, 0, 4)
-    tick("c1", "k1", "z3", "s5")
-    qkv_page(1, 0, 4)
-    tick("c2", "k2", "x3", "z4")
-    qkv_page(2, 0, 4)
-    tick("c3", "x4", "z5", "s6")
+    qkv_page(0, 0, 2)
+    tick("x2", "z4", "c1", "k1")
+    qkv_page(1, 0, 2)
+    tick("h2", "z5", "x3", "c2", "k2")
+    qkv_page(2, 0, 2)
+    tick("h3", "z6")
     keep_wq = pltpu.make_async_copy(wq, wq_out, osem.at[9])
     keep_wq.start()
     for qb in range(4):
@@ -1000,27 +1052,25 @@
             attend_pair(qb, pair, pair, q_ref, k_ref, v_ref, fq, fk, bias, att, linv, mf, p_hbm, stage, psem)
             return 0
 
-        if qb < 2:
-            lax.fori_loop(0, 6, pair_step, 0)
-        else:
-            lax.fori_loop(0, 3, pair_step, 0)
-            tick(*(("c6", "x7", "s9") if qb == 2 else ("c7", "x8")))
-            lax.fori_loop(3, 6, pair_step, 0)
-        drain_pairs(qb, p_hbm, stage, psem)
-        tick(
-            *(
-                ("p3", "c4", "x5", "z6", "s7"),
-                ("k3", "p4", "c5", "x6", "z7", "s8"),
-                ("k5", "p6", "z9"),
-                ("k6", "p7", "x9"),
-            )[qb]
-        )
+        parts = 2 if qb < 2 else 3
+        for part in range(parts):
+            lax.fori_loop(part * 6 // parts, (part + 1) * 6 // parts, pair_step, 0)
+            if part == parts - 1:
+                drain_pairs(qb, p_hbm, stage, psem)
+            tick(
+                *(
+                    (("x4", "z7", "c3"), ("p3",)),
+                    (("x5", "z8", "c4"), ("z9", "k3", "p4")),
+                    (("p5",), ("x7", "c6", "k5"), ()),
+                    (("x8", "c7", "p6"), (), ("x9", "p7", "k6")),
+                )[qb][part]
+            )
         if qb == 1:
             for copy in halo:
                 copy.wait_recv()
             for p in range(3):
-                qkv_page(p, 4, 6)
-            tick("p5", "k4", "z8")
+                qkv_page(p, 2, 3)
+            tick("x6", "c5", "k4")
             saves = [
                 pltpu.make_async_copy(a, b, osem.at[i])
                 for i, (a, b) in enumerate(
@@ -1095,13 +1145,11 @@
     lax.fori_loop(0, 2, back_step, 0)
     for rb in range(4):
         outs.extend(row_copies(rb))
-    ge_ref[0:16] = gao_ref[...].astype(BF)
-    ge_ref[16:48] = gaff_ref[...].astype(BF)
-    ge_ref[48:64] = gbo_ref[...].astype(BF)
-    ge_ref[64:80] = gbdn_ref[...].astype(BF)
-    ge_ref[80:144] = gadn_ref[...].reshape(64, D).astype(BF)
-    ge_ref[144:272] = gbf_ref[...].reshape(128, D).astype(BF)
-    ge_ref[272:288] = tag[...]
+    ge_ref[0:32] = gaff_ref[...].astype(BF)
+    ge_ref[32:48] = gbo_ref[...].astype(BF)
+    ge_ref[48:64] = gbdn_ref[...].astype(BF)
+    ge_ref[64:128] = gadn_ref[...].reshape(64, D).astype(BF)
+    ge_ref[128:256] = gbf_ref[...].reshape(128, D).astype(BF)
     keep_wq.wait()
     for copy in outs:
         copy.wait()
@@ -1112,37 +1160,90 @@
 
 
 def k3_kernel(
-    x_hbm, q_hbm, k_hbm, v_hbm, p_hbm, do_hbm, hf_hbm, ge, lowq_hbm, done_hbm, cos_hbm, sin_hbm,
+    x_hbm, q_hbm, k_hbm, v_hbm, p_hbm, do_hbm, hf_hbm, ge, gao, tag, lowq_hbm, done_hbm, cos_hbm, sin_hbm,
     fq_hbm, fk_hbm, aqkv, bqkv, wq_hbm,
-    dx_ref, sum_e_ref, sum_l_ref,
-    ga_ref, gbq_ref, dproj, eg, lg, ge_in, gl_out, gl_in,
-    xw, q, k, v, do, hf, lowq, done, cos, sin, fq, fk, wq, stage, dq, dkT, dvT, bias, sem, psem, hs, hr, *sems,
+    dx_hbm, gin_ref, gdn_ref, gout_ref, gff_ref,
+    ga_ref, gbq_ref, dproj, eg, lg, e_in, e_half, rs_e, rs_t, gl_out, gl_in, l_half, rs_l, dx_ref,
+    xw, q, k, v, do, hf, lowq, done, cos, sin, fq, fk, wq, stage, dq, dkT, dvT, bias, sem, psem, hs, hr,
+    es, er, ts, tr, ls, lr, dsem, *sems,
 ):
     flip = lax.axis_index("seq")
-    g = Gather(sems)
+    g = Gather(sems, diagonal=(1,))
+
+    def part(src, dst, start, size):
+        return src.at[pl.ds(start, size)], dst.at[pl.ds(start, size)]
+
     table = (
-        (q_hbm, q), (k_hbm, k), (v_hbm, v), (do_hbm, do.at[pl.ds(0, 1024)]), (hf_hbm, hf.at[pl.ds(0, 1024)]),
+        part(q_hbm, q, 0, 256), part(k_hbm, k, 0, 768), part(v_hbm, v, 0, 768), part(do_hbm, do, 0, 256),
+        part(hf_hbm, hf, 0, 1024),
+        part(q_hbm, q, 256, 1280), part(k_hbm, k, 768, 768), part(v_hbm, v, 768, 768), part(do_hbm, do, 256, 768),
         (lowq_hbm, lowq), (done_hbm, done), (cos_hbm, cos), (sin_hbm, sin), (fq_hbm, fq), (fk_hbm, fk), (wq_hbm, wq),
     )
     loads = [pltpu.make_async_copy(a, b, sem.at[i]) for i, (a, b) in enumerate(table)]
     for i in range(4):
         loads.append(
             pltpu.make_async_copy(
-                x_hbm.at[pl.ds(block_at(flip, i), QB)], xw.at[pl.ds(i * QB, QB)], sem.at[12 + i]
+                x_hbm.at[pl.ds(block_at(flip, i), QB)], xw.at[pl.ds(i * QB, QB)], sem.at[16 + i]
             )
         )
     for copy in loads:
         copy.start()
 
-    def early(c, j, half):
-        lanes = slice(None) if half is None else pl.ds(half * 384, 384)
-        return eg.at[j, :, lanes]
-
-    def late(c, j, half):
-        lanes = slice(None) if half is None else pl.ds(half * 384, 384)
-        return lg.at[j, :, lanes]
-
-    g.barrier()
+    def view(c, za, zb, k, half):
+        lanes = ALL if half is None else pl.ds(0, 256) if half == 0 else pl.ds(256, 128)
+        return (eg, lg)[c].at[za, zb, k, :, lanes]
+
+    g.view = view
+
+    def plane(d):
+        return lax.rem(g.b + d, 16)
+
+    def scatter(src, dst, send, recv):
+        def copy(d):
+            to = plane(d)
+            return pltpu.make_async_remote_copy(
+                src(to), dst.at[g.b], send.at[d], recv.at[d], device_id=(to, g.s), device_id_type=MESH
+            )
+
+        def arrival(d):
+            return pltpu.make_async_remote_copy(
+                src(0), dst.at[plane(16 - d)], send.at[d], recv.at[d], device_id=(plane(d), g.s), device_id_type=MESH
+            )
+
+        def each(what):
+            def step(d, _):
+                what(d)
+                return 0
+
+            lax.fori_loop(1, 16, step, 0)
+
+        return (
+            lambda: each(lambda d: copy(d).start()),
+            lambda: each(lambda d: arrival(d).wait_recv()),
+            lambda: each(lambda d: copy(d).wait_send()),
+        )
+
+    def piece(ref, size):
+        def at(to):
+            rows = pl.ds(pl.multiple_of(lax.div(to, 2) * size, size), size)
+            return ref.at[rows, pl.ds(pl.multiple_of(lax.rem(to, 2) * 384, 128), 384)]
+
+        return at
+
+    send_e, wait_e, end_e = scatter(piece(e_half, 16), rs_e, es, er)
+    send_t, wait_t, end_t = scatter(lambda to: tag, rs_t, ts, tr)
+    send_l, wait_l, end_l = scatter(piece(l_half, 8), rs_l, ls, lr)
+
+    bar = pltpu.get_barrier_semaphore()
+
+    def greet(d, _):
+        pl.semaphore_signal(bar, inc=1, device_id=(plane(d), g.s), device_id_type=MESH)
+        return 0
+
+    lax.fori_loop(1, 16, greet, 0)
+    for dev in (g.devy, g.devd):
+        pl.semaphore_signal(bar, inc=1, device_id=dev, device_id_type=MESH)
+    pl.semaphore_wait(bar, 17)
     halo = []
     for i, (src, dst) in enumerate(
         (
@@ -1150,8 +1251,8 @@
             (do_hbm.at[pl.ds(512, QB)], do.at[pl.ds(1280, QB)]),
             (hf_hbm.at[pl.ds(768, QB)], hf.at[pl.ds(1024, QB)]),
             (hf_hbm.at[pl.ds(512, QB)], hf.at[pl.ds(1280, QB)]),
-            (ge.at[pl.ds(pl.multiple_of((1 - flip) * 144, 16), 144)], ge_in),
-            (gl_out.at[pl.ds(pl.multiple_of((1 - flip) * 48, 16), 48)], gl_in),
+            (ge.at[pl.ds(pl.multiple_of((1 - flip) * 128, 16), 128)], e_in),
+            (gl_out.at[pl.ds(pl.multiple_of((1 - flip) * 64, 16), 64)], gl_in),
         )
     ):
         halo.append(
@@ -1161,6 +1262,21 @@
         )
     for copy in (halo[4], halo[0], halo[1], halo[2], halo[3]):
         copy.start()
+    send_t()
+
+    def total_of(ref):
+        totals = [0.0] * ADAPTERS
+        for b in range(16):
+            value = ref[b].astype(F32)
+            for e in range(ADAPTERS):
+                weight = rs_t[b, e : e + 1, :].astype(F32)
+                totals[e] = totals[e] + value * jnp.concatenate([weight] * 3, axis=1)
+        return jnp.concatenate(totals, axis=0).astype(BF)
+
+    def own_piece(ref, size):
+        rows = pl.ds(pl.multiple_of(lax.div(g.b, 2) * size, size), size)
+        return ref[rows, pl.ds(pl.multiple_of(g.core * 384, 128), 384)]
+
     dkT[...] = jnp.zeros_like(dkT)
     dvT[...] = jnp.zeros_like(dvT)
     ga_ref[...] = jnp.zeros_like(ga_ref)
@@ -1184,17 +1300,20 @@
         krows = pl.ds(k0 * QB, n * QB)
 
         def fetch(pair, s, qb=qb, n=n):
-            return pltpu.make_async_copy(p_hbm.at[qb, pair], stage.at[s], psem.at[s])
-
-        fetch(0, 0).start()
+            return prob_copies(n, p_hbm.at[qb, pair], stage.at[s], psem, s)
+
+        for one in fetch(0, 0):
+            one.start()
 
         def pair_step(pair, _, k0=k0, n=n, own=own, rows=rows, krows=krows, fetch=fetch):
             slot = lax.rem(pair, 2)
-            fetch(pair, slot).wait()
+            for one in fetch(pair, slot):
+                one.wait()
 
             @pl.when(pair < 5)
             def _():
-                fetch(pair + 1, 1 - slot).start()
+                for one in fetch(pair + 1, 1 - slot):
+                    one.start()
 
             lanes = pl.ds(pl.multiple_of(pair * 128, 128), 128)
             do2 = do[rows, lanes]
@@ -1206,9 +1325,8 @@
             dqs = []
             for h in range(2):
                 mine = half if h == 1 else jnp.logical_not(half)
-                p = stage[slot, 2 * h, :, 0 : min(D, n * QB)]
-                if n > 3:
-                    p = jnp.concatenate([p, stage[slot, 2 * h + 1, :, 0 : n * QB - D]], axis=1)
+                spots = [divmod(h * n + t, 3) for t in range(n)]
+                p = jnp.concatenate([stage[slot, i, :, j * QB : j * QB + QB] for i, j in spots], axis=1)
                 dp = nt(jnp.where(mine, do2, jnp.zeros_like(do2)), v2)
                 d = ndl[:, h * 128 : (h + 1) * 128]
                 ds = (p.astype(F32) * (dp + jnp.concatenate([d] * (2 * n), axis=1))).astype(BF)
@@ -1221,23 +1339,26 @@
             return 0
 
         lax.fori_loop(0, 6, pair_step, 0)
-        g.view = early
         if qb == 0:
             halo[4].wait_recv()
-            mine = ge[pl.ds(pl.multiple_of(flip * 144, 16), 144)]
-            total = mine.astype(F32) + ge_in[...].astype(F32)
-            row = iota((144, 1), 0)
-            eg[g.me] = jnp.where((row >= 128) & (flip == 1), mine.astype(F32), total).astype(BF)
-            g.stage_own(0)
+            mine = ge[pl.ds(pl.multiple_of(flip * 128, 16), 128), :]
+            e_half[...] = (mine.astype(F32) + e_in[...].astype(F32)).astype(BF)
+            send_e()
+            for copy in loads[5:9]:
+                copy.wait()
         elif qb == 1:
+            rs_e[g.b] = own_piece(e_half, 16)
+            rs_t[g.b] = tag[...]
+            wait_e()
+            wait_t()
+            eg[g.za, g.zb, g.column(0, 0, 0)] = total_of(rs_e)
+            g.send_z(0)
+        elif qb == 2:
             g.stage_z(0)
-        elif qb == 2:
+        else:
             g.stage_xy(0)
-        else:
-            g.stage_corner(0)
-            g.stage_pair(0)
-
-    for copy in loads[5:]:
+
+    for copy in loads[9:]:
         copy.wait()
     for copy in halo[:4]:
         copy.wait_recv()
@@ -1274,23 +1395,7 @@
             return 0
 
         lax.fori_loop(0, 6, halo_step, 0)
-
-    g.stage_core(0)
-
-    def weights_of(b, e):
-        return eg[2 * b + 1, 128 + e : 129 + e, :].astype(F32)
-
-    def sum_step(i, _):
-        y = lax.div(i, 9)
-        r = pl.multiple_of(lax.rem(i, 9) * 16, 16)
-        totals = [jnp.zeros((16, D), F32) for _ in range(ADAPTERS)]
-        for b in range(16):
-            part = eg[2 * b + y, pl.ds(r, 16), :].astype(F32)
-            for e in range(ADAPTERS):
-                totals[e] += part * weights_of(b, e)
-        for e in range(ADAPTERS):
-            sum_e_ref[e, pl.ds(pl.multiple_of(i * 16, 16), 16), :] = totals[e]
-        return 0
+        (g.stage_corner, g.stage_pair)[i](0)
 
     lane = lax.div(iota((1, 48), 1), 16)
     rank = lax.div(iota((48, 1), 0), 16)
@@ -1322,50 +1427,86 @@
     lax.fori_loop(0, 4, proj_step, 0)
     gl_out[0:48] = ga_ref[...].astype(BF)
     gl_out[48:96] = gbq_ref[...].astype(BF)
+    gl_out[96:112] = gao[...].astype(BF)
+    gl_out[112:128] = jnp.zeros((16, D), BF)
     halo[5].start()
-    g.view = late
 
     def dx_rows(rb):
         rows = pl.ds(rb * QB, QB)
         total = done[rows, :] + nn(lowq[rows, :], aqkv[...])
         for p in range(3):
             total += nt(dproj[p, rows, :], wq[p].reshape(D, D))
-        dx_ref[pl.ds(block_at(flip, rb), QB), :] = total.astype(BF)
-
-    lax.fori_loop(0, 18, sum_step, 0)
+        dx_ref[rows, :] = total.astype(BF)
+        copy = pltpu.make_async_copy(dx_ref.at[rows], dx_hbm.at[pl.ds(block_at(flip, rb), QB)], dsem.at[rb])
+        copy.start()
+        return copy
+
+    def blocks(ref):
+        for z in range(4):
+            for xx in range(2):
+                for core in range(2):
+                    for y in range(2):
+                        yield (
+                            y * 8 + z * 2 + xx, core * 384,
+                            ref[z // 2, z % 2, (xx * 2 + core) * 2 + y].astype(F32),
+                        )
+
+    def place_early():
+        for group, lane0, value in blocks(eg):
+            lanes = slice(lane0, lane0 + 384)
+            for e in range(ADAPTERS):
+                rows = value[16 * e : 16 * e + 16]
+                if group < 2:
+                    gin_ref[e, 64 + 16 * group : 80 + 16 * group, lanes] = rows
+                elif group < 4:
+                    gout_ref[e, 16 + 16 * group : 32 + 16 * group, lanes] = rows
+                elif group < 8:
+                    at = (group - 4) * D + lane0
+                    gdn_ref[e, :, at : at + 384] = rows
+                else:
+                    at = (group - 8) // 2 * D + lane0
+                    first = 16 * (group % 2)
+                    gff_ref[e, first : first + 16, at : at + 384] = rows
+
+    def place_late():
+        for group, lane0, value in blocks(lg):
+            lanes = slice(lane0, lane0 + 384)
+            for e in range(ADAPTERS):
+                rows = value[8 * e : 8 * e + 8]
+                if group < 6:
+                    gin_ref[e, 8 * group : 8 * group + 8, lanes] = rows
+                elif group < 12:
+                    gout_ref[e, 8 * group - 48 : 8 * group - 40, lanes] = rows
+                elif group < 14:
+                    gin_ref[e, 8 * group - 48 : 8 * group - 40, lanes] = rows
+
+    tails = [dx_rows(0)]
     halo[5].wait_recv()
-    lg[g.me] = (
-        gl_out[pl.ds(pl.multiple_of(flip * 48, 16), 48)].astype(F32) + gl_in[...].astype(F32)
-    ).astype(BF)
-    g.stage_own(1)
-    dx_rows(0)
+    mine = gl_out[pl.ds(pl.multiple_of(flip * 64, 16), 64), :]
+    l_half[...] = mine.astype(F32) + gl_in[...].astype(F32)
+    send_l()
+    tails.append(dx_rows(1))
+    rs_l[g.b] = own_piece(l_half, 8)
+    wait_l()
+    lg[g.za, g.zb, g.column(0, 0, 0)] = total_of(rs_l)
+    g.send_z(1)
+    tails.append(dx_rows(2))
     g.stage_z(1)
-    dx_rows(1)
+    tails.append(dx_rows(3))
+    g.stage_core(0)
+    place_early()
     g.stage_xy(1)
-    dx_rows(2)
-    g.stage_corner(1)
-    dx_rows(3)
-    g.stage_pair(1)
-    g.stage_core(1)
-
-    def late_step(i, _):
-        y = lax.div(i, 3)
-        r = pl.multiple_of(lax.rem(i, 3) * 16, 16)
-        totals = [jnp.zeros((16, D), F32) for _ in range(ADAPTERS)]
-        for b in range(16):
-            part = lg[2 * b + y, pl.ds(r, 16), :].astype(F32)
-            for e in range(ADAPTERS):
-                totals[e] += part * weights_of(b, e)
-        for e in range(ADAPTERS):
-            sum_l_ref[e, pl.ds(pl.multiple_of(i * 16, 16), 16), :] = totals[e]
-        return 0
-
-    lax.fori_loop(0, 6, late_step, 0)
     for copy in halo:
         copy.wait_send()
-    for c, view in enumerate((early, late)):
-        g.view = view
-        g.finish(c)
+    end_e()
+    end_t()
+    end_l()
+    g.finish(0)
+    g.stage_core(1)
+    place_late()
+    g.finish(1)
+    for copy in tails:
+        copy.wait()
 
 
 def sds(shape, dtype):
@@ -1382,26 +1523,28 @@
         (ANY, (1024, D), BF), (ANY, (1024, D), BF), (INV, (1024, 128), BF),
         (ANY, (1536, 48), BF), (ANY, (1024, D), F32), (ANY, (1536, 128), F32), (ANY, (1536, 128), F32),
         (ANY, (1536, 128), BF), (ANY, (1536, 128), BF),
-        (INV, (288, D), BF), (ANY, (3, 32, 24, D), BF),
+        (INV, (256, D), BF), (INV, (16, D), F32), (INV, (16, 128), BF), (INV, (48, D), BF), (INV, (48, D), BF),
+        (ANY, (3, 2, 2, 8, 24, D), BF),
     ]
     V = pltpu.VMEM
     scratch = [
-        V((16, D), F32), V((32, D), F32), V((4, 16, D), F32), V((16, D), F32), V((16, D), F32), V((4, 32, D), F32),
-        V((3, 32, 24, D), BF), V((32, 24, D), BF), V((4, 2, 32, 24, D), BF), V((32, 96, D), BF),
+        V((16, D), BF), V((16, D), BF), V((32, D), BF), V((4, 16, D), BF), V((16, D), BF), V((4, D), F32),
+        V((32, D), F32), V((4, 16, D), F32), V((16, D), F32), V((16, D), F32), V((4, 32, D), F32),
+        V((3, 2, 2, 8, 24, D), BF), V((2, 2, 8, 24, D), BF), V((4, 2, 2, 2, 8, 24, D), BF), V((2, 2, 8, 96, D), BF),
         V((32, QB, D), BF), V((1536, D), BF), V((1024, D), BF), V((1024, D), F32),
         V((1024, D), F32), V((1024, D), F32), V((1024, D), BF), V((1024, D), BF),
         V((1536, 128), F32), V((1536, 128), F32), V((1536, 128), BF), V((1536, 128), BF), V((2, QB, QB), F32),
         V((1024, 128), F32), V((1536, 48), BF), V((1024, 16), BF), V((1024, 32), BF),
         V((1024, 16), BF), V((512, D), F32), V((512, 32), F32), V((3, 48, D), BF),
         V((4, 32, D), BF), V((4, 32, D), BF), V((D, 128), BF), V((1024, D), BF), V((1024, D), BF),
-        pltpu.SemaphoreType.DMA((9,)), pltpu.SemaphoreType.DMA((7,)), pltpu.SemaphoreType.DMA((8,)), pltpu.SemaphoreType.DMA((10,)),
-        pltpu.SemaphoreType.DMA((2,)), pltpu.SemaphoreType.DMA((2,)), pltpu.SemaphoreType.DMA((2,)),
+        pltpu.SemaphoreType.DMA((9,)), pltpu.SemaphoreType.DMA((10,)), pltpu.SemaphoreType.DMA((7,)), pltpu.SemaphoreType.DMA((8,)), pltpu.SemaphoreType.DMA((10,)),
+        pltpu.SemaphoreType.DMA((4,)), pltpu.SemaphoreType.DMA((4,)), pltpu.SemaphoreType.DMA((4,)),
     ]
     scratch += gather_sems(NCHUNK)
     return pl.pallas_call(
         kf_kernel,
         out_shape=[sds(s, t) for _, s, t in outs],
-        in_specs=[ANY()] * 2 + [INV()] * 12 + [ANY()] * 4,
+        in_specs=[ANY()] * 2 + [INV()] * 2 + [pl.BlockSpec(memory_space=pltpu.SMEM)] + [INV()] * 2 + [ANY()] * 8,
         out_specs=[m() for m, _, _ in outs],
         scratch_shapes=scratch,
         compiler_params=pltpu.CompilerParams(
@@ -1412,22 +1555,25 @@
 
 def k3_call(*args):
     V = pltpu.VMEM
+    S = pltpu.SemaphoreType.DMA
     scratch = [
-        V((48, D), F32), V((48, D), F32), V((3, 1024, D), BF), V((32, 144, D), BF), V((32, 48, D), BF),
-        V((144, D), BF), V((96, D), BF), V((48, D), BF),
+        V((48, D), F32), V((48, D), F32), V((3, 1024, D), BF), V((2, 2, 8, 64, 384), BF), V((2, 2, 8, 32, 384), BF),
+        V((128, D), BF), V((128, D), BF), V((16, 16, 384), BF), V((16, 16, 128), BF), V((128, D), BF), V((64, D), BF),
+        V((64, D), F32), V((16, 8, 384), F32), V((1024, D), BF),
         V((1024, D), BF), V((1536, D), BF), V((1536, D), BF), V((1536, D), BF), V((1536, D), BF), V((1536, 128), BF),
         V((1536, 48), BF), V((1024, D), F32), V((1536, 128), F32), V((1536, 128), F32), V((1536, 128), BF),
-        V((1536, 128), BF), V((3, 32, 24, D), BF), V((2, 4, QB, D), BF), V((1024, D), F32), V((D, 1024), F32),
-        V((D, 1024), F32), V((QB, QB), F32), pltpu.SemaphoreType.DMA((16,)), pltpu.SemaphoreType.DMA((2,)),
-        pltpu.SemaphoreType.DMA((6,)), pltpu.SemaphoreType.DMA((6,)),
+        V((1536, 128), BF), V((3, 2, 2, 8, 24, D), BF), V((2, 4, QB, D), BF), V((1024, D), F32), V((D, 1024), F32),
+        V((D, 1024), F32), V((QB, QB), F32), S((20,)), S((4,)), S((6,)), S((6,)),
+        S((16,)), S((16,)), S((16,)), S((16,)), S((16,)), S((16,)), S((4,)),
     ]
-    scratch += gather_sems(2)
     return pl.pallas_call(
         k3_kernel,
-        out_shape=[sds((1024, D), BF), sds((4, 288, D), F32), sds((4, 96, D), F32)],
-        in_specs=[ANY()] * 7 + [INV()] + [ANY()] * 6 + [INV()] * 2 + [ANY()],
-        out_specs=[INV()] * 3,
-        scratch_shapes=scratch,
+        out_shape=[
+            sds((1024, D), BF), sds((4, 96, D), F32), sds((4, 16, FF), F32), sds((4, 80, D), F32), sds((4, 32, FF), F32),
+        ],
+        in_specs=[ANY()] * 7 + [INV()] * 3 + [ANY()] * 6 + [INV()] * 2 + [ANY()],
+        out_specs=[ANY()] + [INV()] * 4,
+        scratch_shapes=scratch + gather_sems(2),
         compiler_params=pltpu.CompilerParams(
             vmem_limit_bytes=VMEM_LIMIT, collective_id=2, has_side_effects=True
         ),
@@ -1439,30 +1585,21 @@
     norm_gain, norm_bias, adapt_in, adapt_down, adapt_out, adapt_ffn,
 ):
     x = tokens[0]
-    e = adapter_index[0, 0]
-    pick = lambda table: lax.dynamic_index_in_dim(table[0], e, 0, False)
-    a_in = pick(adapt_in).transpose(0, 2, 1)
-    aqkv, ao, aff = a_in[0:3].reshape(48, D), a_in[3], a_in[4:6].reshape(32, D)
-    adn = pick(adapt_down).T.reshape(16, 4, D).transpose(1, 0, 2)
-    b_out = pick(adapt_out)
-    bqkv, bo, bdn = b_out[0:3].reshape(48, D), b_out[3], b_out[4]
-    bff = pick(adapt_ffn).reshape(32, FF)
-    gb = jnp.stack([norm_gain[0, 0], norm_bias[0, 0], norm_gain[0, 1], norm_bias[0, 1]])
-    freq = jnp.power(ROPE_BASE, -2.0 * jnp.arange(HEAD_DIM // 2, dtype=F32) / HEAD_DIM)
-    freq = jnp.tile(freq, 4)[None]
-    tag = jnp.where(jnp.arange(16)[:, None] == e, 1.0, jnp.zeros((1, D))).astype(BF)
-    q, k, v, p, mixed, do, hf, lowq, done, cos, sin, fq, fk, ge, wq = kf_call(
-        x, cotangent[0], segments, freq, aqkv, bqkv, ao, bo, aff, bff, adn, bdn, gb, tag,
+    freq = np.power(np.float32(ROPE_BASE), np.float32(-2.0 / HEAD_DIM) * np.arange(HEAD_DIM // 2, dtype=np.float32))
+    freq = np.tile(freq.astype(np.float32), 4)[None]
+    q, k, v, p, mixed, do, hf, lowq, done, cos, sin, fq, fk, ge, gao, tag, aqkv, bqkv, wq = kf_call(
+        x, cotangent[0], segments, freq, adapter_index, norm_gain[0], norm_bias[0],
+        adapt_in[0].transpose(0, 1, 3, 2).reshape(ADAPTERS, 96, D), adapt_down[0].transpose(0, 2, 1),
+        adapt_out[0].reshape(ADAPTERS, 80, D), adapt_ffn[0].reshape(ADAPTERS, 32, FF),
         qkv_weight[0], out_weight[0], ffn_in_weight[0], ffn_out_weight[0],
     )
     q, k, v = (a.reshape(1536, D) for a in (q, k, v))
-    dx, se, sl = k3_call(x, q, k, v, p, do, hf, ge, lowq, done, cos, sin, fq, fk, aqkv, bqkv, wq)
-    g_in = jnp.concatenate([sl[:, :48], se[:, :48]], axis=1).reshape(4, 6, 16, D)
-    g_dn = se[:, 80:144].reshape(4, 4, 16, D).transpose(0, 2, 1, 3).reshape(4, 16, FF)
-    g_out = jnp.concatenate([sl[:, 48:], se[:, 48:80]], axis=1).reshape(4, 5, 16, D)
-    g_ff = se[:, 144:272].reshape(4, 4, 2, 16, D).transpose(0, 2, 3, 1, 4).reshape(4, 2, 16, FF)
+    dx, g_in, g_dn, g_out, g_ff = k3_call(
+        x, q, k, v, p, do, hf, ge, gao, tag, lowq, done, cos, sin, fq, fk, aqkv, bqkv, wq
+    )
     return (
-        mixed[None], dx[None], g_in.transpose(0, 1, 3, 2)[None], g_dn.transpose(0, 2, 1)[None], g_out[None], g_ff[None],
+        mixed[None], dx[None], g_in.reshape(ADAPTERS, 6, 16, D).transpose(0, 1, 3, 2)[None],
+        g_dn.transpose(0, 2, 1)[None], g_out.reshape(ADAPTERS, 5, 16, D)[None], g_ff.reshape(ADAPTERS, 2, 16, FF)[None],
     )
 
 

time: 328 us -> 271 us (0.83)
  Pallas kernels: 294 us -> 255 us
  local copies, waits for them, and re-layouts: 24.2 us -> 9.14 us
    pallas_call x1, Pallas kernels: 120 us -> 85.3 us  [k3_call(): pl.pallas_call(k3_kernel, out_shape=[sds((1024, D), BF), sds((4, 96, D),...]
    slice x8 -> x0, local copies, waits for them, and re-layouts: 7.73 us -> none  [the longest x1 1.53 us: fast(): se[:, 144:272].reshape(4, 4, 2, 16, D).transpose(0, 2, 3, 1, 4)]
    unnamed x8 -> x16, local copies, waits for them, and re-layouts: 4.44 us -> 9.14 us
    pallas_call x1, Pallas kernels: 174 us -> 170 us  [kf_call(): pl.pallas_call(kf_kernel, out_shape=[sds(s, t) for _, s, t in outs], in_s...]
    another operation x4 -> x0, local copies, waits for them, and re-layouts: 3.35 us -> none  [the longest x1 1.95 us: fast(): g_ff[None]]
where the time goes in v1:
time: 271 us; the launch traced here: 266 us
  Pallas kernels  255 us (94%)
  local copies, waits for them, and re-layouts  9.14 us (3%)
    pallas_call x1, Pallas kernels, kf_call(): pl.pallas_call(kf_kernel, out_shape=[sds(s, t) for _, s, t in outs], in_s...  170 us
    pallas_call x1, Pallas kernels, k3_call(): pl.pallas_call(k3_kernel, out_shape=[sds((1024, D), BF), sds((4, 96, D),...  85.3 us
    unnamed x16, local copies, waits for them, and re-layouts  9.14 us

profile of v1, /device:TPU:1, one launch (start us, length us, event | category | flops | bytes accessed | tf_op | source)
XLA Modules:
  0.0 266.3 jit_solution(12966092722273564838)
XLA Ops:
  1.3 170.0 %shard_map.190 = (bf16[6,256,768]{2,1,0:T(8,128)(2,1)}, bf16[6,256,768]{2,1,0:T(8,128)(2,1)}, bf16[6,256,768]{2,1,0:T(8,128)(2,1)}, bf16[4,6,4,256,768]{4,3,2,1,...) custom-call(bf16[1024,768]{1,0:T(8,128)(2,1)} %bitcast.33, ...), custom_call_target="tpu_custom_call" | custom-call | tf_op jit(solution)/shard_map/pallas_call | solution.py:1544
  171.3 85.3 %shard_map.191 = (bf16[1024,768]{1,0:T(8,128)(2,1)}, f32[4,96,768]{2,1,0:T(8,128)}, f32[4,16,3072]{2,1,0:T(8,128)}, f32[4,80,768]{2,1,0:T(8,128)}, f32[4,32,3072]{2,1,0:T(8,128)}) custom-call(bf16[1024,768]{1,0:T(8,128)(2,1)} %bitcast.34, bf16[1536,768]{1,0:T(8,128)(2,1)} %bitcast.35, bf16[1536,768]{1,0:T(8,128)(2,1)} %bitcast.36, ...), custom_call_target="tpu_custom_call" | custom-call | tf_op jit(solution)/shard_map/pallas_call | solution.py:1569
  256.7 0.0 copy-start.1
  256.7 2.8 %copy.28 = bf16[1,1024,768]{2,1,0:T(8,128)(2,1)} copy(bf16[1,1024,768]{2,1,0:T(8,128)(2,1)} %bitcast.39) | data formatting | bytes 3145728
  259.4 0.0 copy-done.1
  259.4 0.0 copy-start.2
  259.4 1.1 copy.29
  260.6 0.7 copy-done.2
  261.3 0.0 copy-start.4
  261.3 0.0 copy-start.3
  261.3 1.0 copy.30
  262.3 0.5 copy-done.4
  262.8 0.0 copy-start
  262.8 0.9 copy.31
  263.7 0.0 copy-done.3
  263.7 0.9 copy.32
  264.7 0.0 copy-done
  264.7 1.1 copy.33
Async XLA Ops:
  256.7 2.8 %copy-start.1 = (bf16[1024,768]{1,0:T(8,128)(2,1)S(1)}, bf16[1024,768]{1,0:T(8,128)(2,1)}, u32[]{:S(2)}) copy-start(bf16[1024,768]{1,0:T(8,128)(2,1)} %get-tuple-element.49) | copy-start | bytes 4718596
  259.4 1.8 copy-start.2
  261.3 1.6 copy-start.4
  261.3 2.4 copy-start.3
  262.8 1.8 copy-start

commit v2 on v1

--- a/solution.py
+++ b/solution.py
@@ -635,6 +635,13 @@
 HALO_PLAN = ((2, 2), (3, 1))
 NEG = -1e30
 VMEM_LIMIT = int(63.9 * 2**20)
+ORDER = (
+    "h0", "z0", "z1", "z2", "x0", "T", "x1", "x2", "c0", "z4", "h2", "c2", "c1", "k0",
+    "h3", "k2", "z3", "P0", "k1", "x4", "z6", "h1", "P1", "P2", "A003", "z5", "A036", "c4",
+    "A103", "x6", "z7", "A136", "H", "x5", "x3", "p4", "c6", "z8", "A202", "A224", "p6", "c5",
+    "A246", "x7", "c3", "k6", "z9", "A302", "p5", "x8", "c7", "k3", "k4", "A324", "A346", "p7",
+    "k5", "O", "x9", "c8", "k7", "F0", "c9", "p8", "F1", "k8", "p9", "F2", "k9", "F3",
+)
 
 
 def nn(a, b):
@@ -749,11 +756,12 @@
     fq = fq_ref[rows, :]
     keys = jnp.concatenate([k_ref[kblocks, :, lanes].reshape(n * QB, 128), fk_ref[krows, :]], axis=1)
     v2 = v_ref[kblocks, :, lanes].reshape(n * QB, 128)
+    masks = (jnp.logical_not(half), half)
+    scores = [
+        nt(jnp.concatenate([jnp.where(mine, q2, jnp.zeros_like(q2)), fq], axis=1), keys) for mine in masks
+    ]
     outs = []
-    for h in range(2):
-        mine = half if h == 1 else jnp.logical_not(half)
-        qm = jnp.where(mine, q2, jnp.zeros_like(q2))
-        s = nt(jnp.concatenate([qm, fq], axis=1), keys)
+    for h, (mine, s) in enumerate(zip(masks, scores)):
         parts = [s[:, t * QB : (t + 1) * QB] for t in range(n)]
         if tri_last:
             parts[n - 1] = parts[n - 1] + bias_ref[0]
@@ -907,10 +915,11 @@
 
 
 def kf_kernel(
-    x_hbm, cot_hbm, seg_ref, freq_ref, pick_ref, gain_ref, shift_ref, tin_hbm, tdn_hbm, tout_hbm, tff_hbm,
+    x_hbm, cot_hbm, seg_hbm, freq_hbm, pick_hbm, gain_hbm, shift_hbm, tin_hbm, tdn_hbm, tout_hbm, tff_hbm,
     wq_hbm, wo_hbm, wi_hbm, wd_hbm,
-    q_hbm, k_hbm, v_hbm, p_hbm, mixed_hbm, do_hbm, hf_ref, lowq_hbm, done_hbm, cos_hbm, sin_hbm, fq_hbm, fk_hbm,
-    ge_ref, gao_ref, tag_ref, aqkv, bqkv, wq_out,
+    q_hbm, k_hbm, v_hbm, p_hbm, mixed_hbm, do_hbm, hf_hbm, lowq_hbm, done_hbm, cos_hbm, sin_hbm, fq_hbm, fk_hbm,
+    ge_hbm, gao_hbm, tag_hbm, aqkv_hbm, bqkv_hbm, wq_out,
+    seg_ref, freq_ref, pick_ref, gain_ref, shift_ref, hf_ref, ge_ref, gao_ref, tag_ref, aqkv, bqkv, ssem, fsem,
     ao, bo, aff, adn, bdn, gb,
     gaff_ref, gadn_ref, gbo_ref, gbdn_ref, gbf_ref,
     wq, wo, wi, wd, big, xw, att, linv, xhat, dtwo, act, db2, cos, sin, fq, fk, bias, mf,
@@ -932,6 +941,20 @@
                 cot_hbm.at[pl.ds(block_at(flip, i), QB)], cot.at[pl.ds(i * QB, QB)], xsem.at[4 + i]
             )
         )
+    small = [
+        pltpu.make_async_copy(a, b, ssem.at[i])
+        for i, (a, b) in enumerate(
+            ((seg_hbm, seg_ref), (freq_hbm, freq_ref), (pick_hbm, pick_ref), (gain_hbm, gain_ref), (shift_hbm, shift_ref))
+        )
+    ]
+    for copy in small:
+        copy.start()
+    facts = [
+        pltpu.make_async_copy(a, b, fsem.at[i])
+        for i, (a, b) in enumerate(
+            ((tag_ref, tag_hbm), (aqkv, aqkv_hbm), (bqkv, bqkv_hbm), (ge_ref, ge_hbm), (gao_ref, gao_hbm))
+        )
+    ]
     tables = [
         (tin_hbm, big.at[pl.ds(0, ADAPTERS), pl.ds(0, 96)]),
         (tout_hbm, big.at[pl.ds(4, ADAPTERS), pl.ds(0, 80)]),
@@ -941,10 +964,10 @@
         tables.append((tdn_hbm.at[:, :, lanes], big.at[pl.ds(8, ADAPTERS), pl.ds(16 * n, 16)]))
         tables.append((tff_hbm.at[:, :, lanes], big.at[pl.ds(12, ADAPTERS), pl.ds(32 * n, 32)]))
     tables = [pltpu.make_async_copy(a, b, tsem.at[i]) for i, (a, b) in enumerate(tables)]
-    g = Gather(sems, direct=(0, 1, 2))
+    g = Gather(sems, direct=(0, 1, 2, 3))
 
     def view(c, za, zb, k, half):
-        cut = 384 if c < 3 else 640
+        cut = 384 if c < 4 else 640
         lanes = ALL if half is None else pl.ds(0, cut) if half == 0 else pl.ds(cut, D - cut)
         if c < 3:
             return wq.at[c, za, zb, k, :, lanes]
@@ -982,54 +1005,58 @@
         "z": g.stage_z, "x": g.stage_xy, "c": g.stage_corner, "p": g.stage_pair, "k": g.stage_core,
     }
 
-    def tick(*steps):
-        for step in steps:
-            if step[0] == "h":
-                halo[int(step[1])].start()
-            else:
-                kinds[step[0]](int(step[1]))
-
-    tick("h0")
     for copy in loads + tables:
         copy.start()
-    fill_tables(flip, seg_ref, freq_ref, cos, sin, fq, fk, bias)
-    for copy in tables:
-        copy.wait()
-    e = pick_ref[0, 0]
-    aqkv[...] = big[e, 0:48, :]
-    ao[...] = big[e, 48:64, :]
-    aff[...] = big[e, 64:96, :]
-    bqkv[...] = big[4 + e, 0:48, :]
-    bo[...] = big[4 + e, 48:64, :]
-    bdn[...] = big[4 + e, 64:80, :]
-    for n in range(4):
-        adn[n] = big[8 + e, 16 * n : 16 * n + 16, :]
-    tag_ref[...] = jnp.where(iota((16, 128), 0) == e, 1.0, 0.0).astype(BF)
-    for i in range(2):
-        gb[2 * i : 2 * i + 1, :] = gain_ref[i : i + 1, :]
-        gb[2 * i + 1 : 2 * i + 2, :] = shift_ref[i : i + 1, :]
-    rank = iota((48, 1), 0)
-    for p in range(3):
-        keep = (rank >= 16 * p) & (rank < 16 * p + 16)
-        bblk[p] = jnp.where(keep, bqkv[...], jnp.zeros_like(bqkv[...]))
-    rank = iota((32, 1), 0)
-    for n in range(4):
-        piece = big[12 + e, 32 * n : 32 * n + 32, :]
-        bg[n] = jnp.where(rank < 16, piece, jnp.zeros_like(piece))
-        bu[n] = jnp.where(rank >= 16, piece, jnp.zeros_like(piece))
-    head = lax.div(iota((D, 128), 0), HEAD_DIM)
-    spot = iota((D, 128), 1)
-    h2[...] = jnp.where(lax.div(spot - 40, 2) == head, jnp.where(spot >= 40, -1.0, 0.0), 0.0).astype(BF)
-    mf[...] = jnp.zeros_like(mf)
-    dtwo[...] = jnp.zeros_like(dtwo)
-    for ref in (gao_ref, gaff_ref, gadn_ref, gbo_ref, gbdn_ref, gbf_ref):
-        ref[...] = jnp.zeros_like(ref)
-    tick("z0", "z1", "x0", "z2", "x1", "h1", "z3")
-    for copy in loads:
-        copy.wait()
-    tick("c0", "k0")
+
+    def prepare():
+        for copy in small:
+            copy.wait()
+        fill_tables(flip, seg_ref, freq_ref, cos, sin, fq, fk, bias)
+        for copy in tables:
+            copy.wait()
+        e = pick_ref[0, 0]
+        aqkv[...] = big[e, 0:48, :]
+        ao[...] = big[e, 48:64, :]
+        aff[...] = big[e, 64:96, :]
+        bqkv[...] = big[4 + e, 0:48, :]
+        bo[...] = big[4 + e, 48:64, :]
+        bdn[...] = big[4 + e, 64:80, :]
+        for n in range(4):
+            adn[n] = big[8 + e, 16 * n : 16 * n + 16, :]
+        tag_ref[...] = jnp.where(iota((16, 128), 0) == e, 1.0, 0.0).astype(BF)
+        for copy in facts[:3]:
+            copy.start()
+        for i in range(2):
+            gb[2 * i : 2 * i + 1, :] = gain_ref[i : i + 1, :]
+            gb[2 * i + 1 : 2 * i + 2, :] = shift_ref[i : i + 1, :]
+        rank = iota((48, 1), 0)
+        for p in range(3):
+            keep = (rank >= 16 * p) & (rank < 16 * p + 16)
+            bblk[p] = jnp.where(keep, bqkv[...], jnp.zeros_like(bqkv[...]))
+        rank = iota((32, 1), 0)
+        for n in range(4):
+            piece = big[12 + e, 32 * n : 32 * n + 32, :]
+            bg[n] = jnp.where(rank < 16, piece, jnp.zeros_like(piece))
+            bu[n] = jnp.where(rank >= 16, piece, jnp.zeros_like(piece))
+        head = lax.div(iota((D, 128), 0), HEAD_DIM)
+        spot = iota((D, 128), 1)
+        h2[...] = jnp.where(lax.div(spot - 40, 2) == head, jnp.where(spot >= 40, -1.0, 0.0), 0.0).astype(BF)
+        mf[...] = jnp.zeros_like(mf)
+        dtwo[...] = jnp.zeros_like(dtwo)
+        for ref in (gao_ref, gaff_ref, gadn_ref, gbo_ref, gbdn_ref, gbf_ref):
+            ref[...] = jnp.zeros_like(ref)
+        for copy in loads:
+            copy.wait()
+
     q_ref, k_ref, v_ref = (big.at[pl.ds(i * 6, 6)] for i in range(3))
     stage = big.at[pl.ds(18, 8)]
+    keep_wq = pltpu.make_async_copy(wq, wq_out, osem.at[9])
+    saves = [
+        pltpu.make_async_copy(a, b, osem.at[i])
+        for i, (a, b) in enumerate(
+            ((q_ref, q_hbm), (k_ref, k_hbm), (v_ref, v_hbm), (lowq, lowq_hbm), (cos, cos_hbm), (sin, sin_hbm), (fq, fq_hbm), (fk, fk_hbm))
+        )
+    ]
 
     def qkv_page(p, first, last):
         def step(rb, _):
@@ -1038,69 +1065,51 @@
 
         lax.fori_loop(first, last, step, 0)
 
-    qkv_page(0, 0, 2)
-    tick("x2", "z4", "c1", "k1")
-    qkv_page(1, 0, 2)
-    tick("h2", "z5", "x3", "c2", "k2")
-    qkv_page(2, 0, 2)
-    tick("h3", "z6")
-    keep_wq = pltpu.make_async_copy(wq, wq_out, osem.at[9])
-    keep_wq.start()
-    for qb in range(4):
-
-        def pair_step(pair, _, qb=qb):
+    def attend(qb, first, last):
+        def pair_step(pair, _):
             attend_pair(qb, pair, pair, q_ref, k_ref, v_ref, fq, fk, bias, att, linv, mf, p_hbm, stage, psem)
             return 0
 
-        parts = 2 if qb < 2 else 3
-        for part in range(parts):
-            lax.fori_loop(part * 6 // parts, (part + 1) * 6 // parts, pair_step, 0)
-            if part == parts - 1:
-                drain_pairs(qb, p_hbm, stage, psem)
-            tick(
-                *(
-                    (("x4", "z7", "c3"), ("p3",)),
-                    (("x5", "z8", "c4"), ("z9", "k3", "p4")),
-                    (("p5",), ("x7", "c6", "k5"), ()),
-                    (("x8", "c7", "p6"), (), ("x9", "p7", "k6")),
-                )[qb][part]
-            )
-        if qb == 1:
+        lax.fori_loop(first, last, pair_step, 0)
+        if last == 6:
+            drain_pairs(qb, p_hbm, stage, psem)
+
+    def out_step(rb, _):
+        out_rows(rb, xw, att, wo, ao, bo, gb, aff, xhat, rstd, act, lowo, lowf)
+        return 0
+
+    def in_step(i, _):
+        ffn_in_tile(lax.div(i, 2), lax.rem(i, 2), 512, act, lowf, wi, wd, bg, bu, adn, big, lowd, dtwo)
+        return 0
+
+    for step in ORDER:
+        kind, rest = step[0], step[1:]
+        if kind in kinds:
+            kinds[kind](int(rest))
+        elif kind == "h":
+            halo[int(rest)].start()
+        elif step == "T":
+            prepare()
+        elif kind == "P":
+            qkv_page(int(rest), 0, 2)
+        elif step == "H":
             for copy in halo:
                 copy.wait_recv()
             for p in range(3):
                 qkv_page(p, 2, 3)
-            tick("x6", "c5", "k4")
-            saves = [
-                pltpu.make_async_copy(a, b, osem.at[i])
-                for i, (a, b) in enumerate(
-                    ((q_ref, q_hbm), (k_ref, k_hbm), (v_ref, v_hbm), (lowq, lowq_hbm), (cos, cos_hbm), (sin, sin_hbm), (fq, fq_hbm), (fk, fk_hbm))
-                )
-            ]
             for copy in saves:
                 copy.start()
-    for copy in saves:
-        copy.wait()
-    lowd[...] = jnp.zeros_like(lowd)
-
-    def out_step(rb, _):
-        out_rows(rb, xw, att, wo, ao, bo, gb, aff, xhat, rstd, act, lowo, lowf)
-        return 0
-
-    lax.fori_loop(0, 4, out_step, 0)
-    tick("c8")
-
-    def in_step(i, _):
-        ffn_in_tile(lax.div(i, 2), lax.rem(i, 2), 512, act, lowf, wi, wd, bg, bu, adn, big, lowd, dtwo)
-        return 0
-
-    lax.fori_loop(0, 2, in_step, 0)
-    tick("k7", "p8", "c9")
-    lax.fori_loop(2, 4, in_step, 0)
-    tick("k8", "p9")
-    lax.fori_loop(4, 6, in_step, 0)
-    tick("k9")
-    lax.fori_loop(6, 8, in_step, 0)
+            keep_wq.start()
+        elif kind == "A":
+            attend(*(int(v) for v in rest))
+        elif step == "O":
+            for copy in saves:
+                copy.wait()
+            lowd[...] = jnp.zeros_like(lowd)
+            lax.fori_loop(0, 4, out_step, 0)
+        elif kind == "F":
+            n = int(rest)
+            lax.fori_loop(2 * n, 2 * n + 2, in_step, 0)
 
     def down_step(rb, _):
         ffn_out_rows(rb, flip, lowd, bdn, xhat, gb, cot, dtwo, db2, dlow, mixed_ref, gbdn_ref)
@@ -1115,6 +1124,7 @@
         return (
             pltpu.make_async_copy(do_ref.at[rows], do_hbm.at[rows], rsem.at[1 + rb]),
             pltpu.make_async_copy(dtwo.at[rows], done_hbm.at[rows], rsem.at[5 + rb]),
+            pltpu.make_async_copy(hf_ref.at[rows], hf_hbm.at[rows], rsem.at[9 + rb]),
         )
 
     def back_step(half, _):
@@ -1150,8 +1160,10 @@
     ge_ref[48:64] = gbdn_ref[...].astype(BF)
     ge_ref[64:128] = gadn_ref[...].reshape(64, D).astype(BF)
     ge_ref[128:256] = gbf_ref[...].reshape(128, D).astype(BF)
+    for copy in facts[3:]:
+        copy.start()
     keep_wq.wait()
-    for copy in outs:
+    for copy in outs + facts:
         copy.wait()
     for copy in halo:
         copy.wait_send()
@@ -1160,9 +1172,10 @@
 
 
 def k3_kernel(
-    x_hbm, q_hbm, k_hbm, v_hbm, p_hbm, do_hbm, hf_hbm, ge, gao, tag, lowq_hbm, done_hbm, cos_hbm, sin_hbm,
-    fq_hbm, fk_hbm, aqkv, bqkv, wq_hbm,
-    dx_hbm, gin_ref, gdn_ref, gout_ref, gff_ref,
+    x_hbm, q_hbm, k_hbm, v_hbm, p_hbm, do_hbm, hf_hbm, ge_hbm, gao_hbm, tag_hbm, lowq_hbm, done_hbm, cos_hbm, sin_hbm,
+    fq_hbm, fk_hbm, aqkv_hbm, bqkv_hbm, wq_hbm,
+    dx_hbm, eg_hbm, lg_hbm,
+    ge, gao, tag, aqkv, bqkv, gsem,
     ga_ref, gbq_ref, dproj, eg, lg, e_in, e_half, rs_e, rs_t, gl_out, gl_in, l_half, rs_l, dx_ref,
     xw, q, k, v, do, hf, lowq, done, cos, sin, fq, fk, wq, stage, dq, dkT, dvT, bias, sem, psem, hs, hr,
     es, er, ts, tr, ls, lr, dsem, *sems,
@@ -1177,13 +1190,14 @@
         part(q_hbm, q, 0, 256), part(k_hbm, k, 0, 768), part(v_hbm, v, 0, 768), part(do_hbm, do, 0, 256),
         part(hf_hbm, hf, 0, 1024),
         part(q_hbm, q, 256, 1280), part(k_hbm, k, 768, 768), part(v_hbm, v, 768, 768), part(do_hbm, do, 256, 768),
+        (ge_hbm, ge), (tag_hbm, tag), (gao_hbm, gao), (aqkv_hbm, aqkv), (bqkv_hbm, bqkv),
         (lowq_hbm, lowq), (done_hbm, done), (cos_hbm, cos), (sin_hbm, sin), (fq_hbm, fq), (fk_hbm, fk), (wq_hbm, wq),
     )
     loads = [pltpu.make_async_copy(a, b, sem.at[i]) for i, (a, b) in enumerate(table)]
     for i in range(4):
         loads.append(
             pltpu.make_async_copy(
-                x_hbm.at[pl.ds(block_at(flip, i), QB)], xw.at[pl.ds(i * QB, QB)], sem.at[16 + i]
+                x_hbm.at[pl.ds(block_at(flip, i), QB)], xw.at[pl.ds(i * QB, QB)], sem.at[21 + i]
             )
         )
     for copy in loads:
@@ -1230,6 +1244,8 @@
 
         return at
 
+    loads[9].wait()
+    loads[10].wait()
     send_e, wait_e, end_e = scatter(piece(e_half, 16), rs_e, es, er)
     send_t, wait_t, end_t = scatter(lambda to: tag, rs_t, ts, tr)
     send_l, wait_l, end_l = scatter(piece(l_half, 8), rs_l, ls, lr)
@@ -1323,18 +1339,18 @@
             qT = q[rows, lanes].T
             doT = do2.T
             dqs = []
-            for h in range(2):
-                mine = half if h == 1 else jnp.logical_not(half)
+            masks = (jnp.logical_not(half), half)
+            dps = [nt(jnp.where(mine, do2, jnp.zeros_like(do2)), v2) for mine in masks]
+            for h, dp in enumerate(dps):
                 spots = [divmod(h * n + t, 3) for t in range(n)]
                 p = jnp.concatenate([stage[slot, i, :, j * QB : j * QB + QB] for i, j in spots], axis=1)
-                dp = nt(jnp.where(mine, do2, jnp.zeros_like(do2)), v2)
                 d = ndl[:, h * 128 : (h + 1) * 128]
                 ds = (p.astype(F32) * (dp + jnp.concatenate([d] * (2 * n), axis=1))).astype(BF)
-                dqs.append(nn(ds, k2))
                 hr = pl.ds(pl.multiple_of(pair * 128 + h * 64, 64), 64)
                 kc = pl.ds(k0 * QB, own * QB)
+                dvT[hr, kc] += nn(doT[h * 64 : (h + 1) * 64], p[:, 0 : own * QB])
+                dqs.append(nn(ds, k2))
                 dkT[hr, kc] += nn(qT[h * 64 : (h + 1) * 64], ds[:, 0 : own * QB])
-                dvT[hr, kc] += nn(doT[h * 64 : (h + 1) * 64], p[:, 0 : own * QB])
             dq[rows, lanes] = jnp.where(half, dqs[1], dqs[0]) * 0.125
             return 0
 
@@ -1358,44 +1374,48 @@
         else:
             g.stage_xy(0)
 
-    for copy in loads[9:]:
+    for copy in loads[11:]:
         copy.wait()
     for copy in halo[:4]:
         copy.wait_recv()
-    for i, (k0, n) in enumerate(HALO_PLAN):
-        rows = pl.ds(1024 + i * QB, QB)
-        krows = pl.ds(k0 * QB, n * QB)
-
-        def halo_step(pair, _, k0=k0, n=n, rows=rows, krows=krows):
-            lanes = pl.ds(pl.multiple_of(pair * 128, 128), 128)
+    def halo_step(pair, _):
+        lanes = pl.ds(pl.multiple_of(pair * 128, 128), 128)
+        delta_picks = picks(pair, 40, 2)
+        top_picks = picks(pair, 4, 3)
+        masks = (jnp.logical_not(half), half)
+        work = []
+        for i, (k0, n) in enumerate(HALO_PLAN):
+            rows = pl.ds(1024 + i * QB, QB)
+            krows = pl.ds(k0 * QB, n * QB)
             do2 = do[rows, lanes]
             q2 = q[rows, lanes]
             feats = hf[rows, :]
-            ndl = nn(feats, picks(pair, 40, 2))
-            nm = nn(feats, picks(pair, 4, 3))
+            ndl = nn(feats, delta_picks)
+            nm = nn(feats, top_picks)
             keys = jnp.concatenate([k[krows, lanes], fk[krows, :]], axis=1)
             v2 = v[krows, lanes]
-            qT = q2.T
-            doT = do2.T
-            for h in range(2):
-                mine = half if h == 1 else jnp.logical_not(half)
+            for h, mine in enumerate(masks):
                 s = nt(jnp.concatenate([jnp.where(mine, q2, jnp.zeros_like(q2)), fq[rows, :]], axis=1), keys)
-                parts = [s[:, t * QB : (t + 1) * QB] for t in range(n)]
-                parts[0] = parts[0] + bias[...]
-                s = jnp.concatenate(parts, axis=1)
-                m = nm[:, h * 128 : (h + 1) * 128]
-                p = jnp.exp(s + jnp.concatenate([m] * (2 * n), axis=1))
                 dp = nt(jnp.where(mine, do2, jnp.zeros_like(do2)), v2)
-                d = ndl[:, h * 128 : (h + 1) * 128]
-                ds = (p * (dp + jnp.concatenate([d] * (2 * n), axis=1))).astype(BF)
-                hr = pl.ds(pl.multiple_of(pair * 128 + h * 64, 64), 64)
-                kc = pl.ds(k0 * QB, n * QB)
-                dkT[hr, kc] += nn(qT[h * 64 : (h + 1) * 64], ds)
-                dvT[hr, kc] += nn(doT[h * 64 : (h + 1) * 64], p.astype(BF))
-            return 0
-
-        lax.fori_loop(0, 6, halo_step, 0)
-        (g.stage_corner, g.stage_pair)[i](0)
+                work.append((k0, n, h, s, dp, nm, ndl, q2.T, do2.T))
+        for k0, n, h, s, dp, nm, ndl, qT, doT in work:
+            parts = [s[:, t * QB : (t + 1) * QB] for t in range(n)]
+            parts[0] = parts[0] + bias[...]
+            s = jnp.concatenate(parts, axis=1)
+            m = nm[:, h * 128 : (h + 1) * 128]
+            p = jnp.exp(s + jnp.concatenate([m] * (2 * n), axis=1))
+            d = ndl[:, h * 128 : (h + 1) * 128]
+            ds = (p * (dp + jnp.concatenate([d] * (2 * n), axis=1))).astype(BF)
+            hr = pl.ds(pl.multiple_of(pair * 128 + h * 64, 64), 64)
+            kc = pl.ds(k0 * QB, n * QB)
+            dvT[hr, kc] += nn(doT[h * 64 : (h + 1) * 64], p.astype(BF))
+            dkT[hr, kc] += nn(qT[h * 64 : (h + 1) * 64], ds)
+        return 0
+
+    lax.fori_loop(0, 3, halo_step, 0)
+    g.stage_corner(0)
+    lax.fori_loop(3, 6, halo_step, 0)
+    g.stage_pair(0)
 
     lane = lax.div(iota((1, 48), 1), 16)
     rank = lax.div(iota((48, 1), 0), 16)
@@ -1441,45 +1461,6 @@
         copy.start()
         return copy
 
-    def blocks(ref):
-        for z in range(4):
-            for xx in range(2):
-                for core in range(2):
-                    for y in range(2):
-                        yield (
-                            y * 8 + z * 2 + xx, core * 384,
-                            ref[z // 2, z % 2, (xx * 2 + core) * 2 + y].astype(F32),
-                        )
-
-    def place_early():
-        for group, lane0, value in blocks(eg):
-            lanes = slice(lane0, lane0 + 384)
-            for e in range(ADAPTERS):
-                rows = value[16 * e : 16 * e + 16]
-                if group < 2:
-                    gin_ref[e, 64 + 16 * group : 80 + 16 * group, lanes] = rows
-                elif group < 4:
-                    gout_ref[e, 16 + 16 * group : 32 + 16 * group, lanes] = rows
-                elif group < 8:
-                    at = (group - 4) * D + lane0
-                    gdn_ref[e, :, at : at + 384] = rows
-                else:
-                    at = (group - 8) // 2 * D + lane0
-                    first = 16 * (group % 2)
-                    gff_ref[e, first : first + 16, at : at + 384] = rows
-
-    def place_late():
-        for group, lane0, value in blocks(lg):
-            lanes = slice(lane0, lane0 + 384)
-            for e in range(ADAPTERS):
-                rows = value[8 * e : 8 * e + 8]
-                if group < 6:
-                    gin_ref[e, 8 * group : 8 * group + 8, lanes] = rows
-                elif group < 12:
-                    gout_ref[e, 8 * group - 48 : 8 * group - 40, lanes] = rows
-                elif group < 14:
-                    gin_ref[e, 8 * group - 48 : 8 * group - 40, lanes] = rows
-
     tails = [dx_rows(0)]
     halo[5].wait_recv()
     mine = gl_out[pl.ds(pl.multiple_of(flip * 64, 16), 64), :]
@@ -1494,7 +1475,8 @@
     g.stage_z(1)
     tails.append(dx_rows(3))
     g.stage_core(0)
-    place_early()
+    keep_e = pltpu.make_async_copy(eg, eg_hbm, gsem.at[0])
+    keep_e.start()
     g.stage_xy(1)
     for copy in halo:
         copy.wait_send()
@@ -1503,9 +1485,79 @@
     end_l()
     g.finish(0)
     g.stage_core(1)
-    place_late()
+    keep_l = pltpu.make_async_copy(lg, lg_hbm, gsem.at[1])
+    keep_l.start()
     g.finish(1)
+    keep_e.wait()
+    keep_l.wait()
     for copy in tails:
+        copy.wait()
+
+
+def k4_kernel(
+    eg_hbm, lg_hbm, mixed_hbm, dx_hbm,
+    mixed_out, dx_out, gin_hbm, gdn_hbm, gout_hbm, gff_hbm,
+    eg, lg, gin_ref, gdn_ref, gout_ref, gff_ref, mixed, dx, sem,
+):
+    moves = [
+        pltpu.make_async_copy(a, b, sem.at[i])
+        for i, (a, b) in enumerate(
+            (
+                (eg_hbm, eg), (lg_hbm, lg), (mixed_hbm, mixed), (dx_hbm, dx),
+                (gdn_ref, gdn_hbm), (gff_ref, gff_hbm), (gin_ref, gin_hbm), (gout_ref, gout_hbm),
+                (mixed, mixed_out), (dx, dx_out),
+            )
+        )
+    ]
+    for copy in moves[:4]:
+        copy.start()
+
+    def blocks(ref):
+        for z in range(4):
+            for xx in range(2):
+                for core in range(2):
+                    for y in range(2):
+                        yield (
+                            y * 8 + z * 2 + xx, core * 384,
+                            ref[z // 2, z % 2, (xx * 2 + core) * 2 + y].astype(F32),
+                        )
+
+    moves[0].wait()
+    for group, lane0, value in blocks(eg):
+        lanes = slice(lane0, lane0 + 384)
+        for e in range(ADAPTERS):
+            rows = value[16 * e : 16 * e + 16]
+            if group < 2:
+                gin_ref[e, 64 + 16 * group : 80 + 16 * group, lanes] = rows
+            elif group < 4:
+                gout_ref[e, 16 + 16 * group : 32 + 16 * group, lanes] = rows
+            elif group < 8:
+                at = (group - 4) * D + lane0
+                gdn_ref[e, :, at : at + 384] = rows
+            else:
+                at = (group - 8) // 2 * D + lane0
+                first = 16 * (group % 2)
+                gff_ref[e, first : first + 16, at : at + 384] = rows
+
+    for i in (2, 3):
+        moves[i].wait()
+    for i in (4, 5, 8, 9):
+        moves[i].start()
+    moves[1].wait()
+    for group, lane0, value in blocks(lg):
+        lanes = slice(lane0, lane0 + 384)
+        for e in range(ADAPTERS):
+            rows = value[8 * e : 8 * e + 8]
+            if group < 6:
+                gin_ref[e, 8 * group : 8 * group + 8, lanes] = rows
+            elif group < 12:
+                gout_ref[e, 8 * group - 48 : 8 * group - 40, lanes] = rows
+            elif group < 14:
+                gin_ref[e, 8 * group - 48 : 8 * group - 40, lanes] = rows
+
+    for copy in moves[6:8]:
+        copy.start()
+    for copy in moves[4:]:
         copy.wait()
 
 
@@ -1520,14 +1572,17 @@
 def kf_call(*args):
     outs = [
         (ANY, (6, QB, D), BF), (ANY, (6, QB, D), BF), (ANY, (6, QB, D), BF), (ANY, (4, 6, 4, QB, D), BF),
-        (ANY, (1024, D), BF), (ANY, (1024, D), BF), (INV, (1024, 128), BF),
+        (ANY, (1024, D), BF), (ANY, (1024, D), BF), (ANY, (1024, 128), BF),
         (ANY, (1536, 48), BF), (ANY, (1024, D), F32), (ANY, (1536, 128), F32), (ANY, (1536, 128), F32),
         (ANY, (1536, 128), BF), (ANY, (1536, 128), BF),
-        (INV, (256, D), BF), (INV, (16, D), F32), (INV, (16, 128), BF), (INV, (48, D), BF), (INV, (48, D), BF),
+        (ANY, (256, D), BF), (ANY, (16, D), F32), (ANY, (16, 128), BF), (ANY, (48, D), BF), (ANY, (48, D), BF),
         (ANY, (3, 2, 2, 8, 24, D), BF),
     ]
     V = pltpu.VMEM
     scratch = [
+        V((1, 2048), jnp.int32), V((1, 128), F32), pltpu.SMEM((1, 1), jnp.int32), V((2, D), F32), V((2, D), F32),
+        V((1024, 128), BF), V((256, D), BF), V((16, D), F32), V((16, 128), BF), V((48, D), BF), V((48, D), BF),
+        pltpu.SemaphoreType.DMA((5,)), pltpu.SemaphoreType.DMA((5,)),
         V((16, D), BF), V((16, D), BF), V((32, D), BF), V((4, 16, D), BF), V((16, D), BF), V((4, D), F32),
         V((32, D), F32), V((4, 16, D), F32), V((16, D), F32), V((16, D), F32), V((4, 32, D), F32),
         V((3, 2, 2, 8, 24, D), BF), V((2, 2, 8, 24, D), BF), V((4, 2, 2, 2, 8, 24, D), BF), V((2, 2, 8, 96, D), BF),
@@ -1537,14 +1592,14 @@
         V((1024, 128), F32), V((1536, 48), BF), V((1024, 16), BF), V((1024, 32), BF),
         V((1024, 16), BF), V((512, D), F32), V((512, 32), F32), V((3, 48, D), BF),
         V((4, 32, D), BF), V((4, 32, D), BF), V((D, 128), BF), V((1024, D), BF), V((1024, D), BF),
-        pltpu.SemaphoreType.DMA((9,)), pltpu.SemaphoreType.DMA((10,)), pltpu.SemaphoreType.DMA((7,)), pltpu.SemaphoreType.DMA((8,)), pltpu.SemaphoreType.DMA((10,)),
+        pltpu.SemaphoreType.DMA((13,)), pltpu.SemaphoreType.DMA((10,)), pltpu.SemaphoreType.DMA((7,)), pltpu.SemaphoreType.DMA((8,)), pltpu.SemaphoreType.DMA((10,)),
         pltpu.SemaphoreType.DMA((4,)), pltpu.SemaphoreType.DMA((4,)), pltpu.SemaphoreType.DMA((4,)),
     ]
     scratch += gather_sems(NCHUNK)
     return pl.pallas_call(
         kf_kernel,
         out_shape=[sds(s, t) for _, s, t in outs],
-        in_specs=[ANY()] * 2 + [INV()] * 2 + [pl.BlockSpec(memory_space=pltpu.SMEM)] + [INV()] * 2 + [ANY()] * 8,
+        in_specs=[ANY()] * 15,
         out_specs=[m() for m, _, _ in outs],
         scratch_shapes=scratch,
         compiler_params=pltpu.CompilerParams(
@@ -1557,26 +1612,42 @@
     V = pltpu.VMEM
     S = pltpu.SemaphoreType.DMA
     scratch = [
+        V((256, D), BF), V((16, D), F32), V((16, 128), BF), V((48, D), BF), V((48, D), BF), S((2,)),
         V((48, D), F32), V((48, D), F32), V((3, 1024, D), BF), V((2, 2, 8, 64, 384), BF), V((2, 2, 8, 32, 384), BF),
         V((128, D), BF), V((128, D), BF), V((16, 16, 384), BF), V((16, 16, 128), BF), V((128, D), BF), V((64, D), BF),
         V((64, D), F32), V((16, 8, 384), F32), V((1024, D), BF),
         V((1024, D), BF), V((1536, D), BF), V((1536, D), BF), V((1536, D), BF), V((1536, D), BF), V((1536, 128), BF),
         V((1536, 48), BF), V((1024, D), F32), V((1536, 128), F32), V((1536, 128), F32), V((1536, 128), BF),
         V((1536, 128), BF), V((3, 2, 2, 8, 24, D), BF), V((2, 4, QB, D), BF), V((1024, D), F32), V((D, 1024), F32),
-        V((D, 1024), F32), V((QB, QB), F32), S((20,)), S((4,)), S((6,)), S((6,)),
+        V((D, 1024), F32), V((QB, QB), F32), S((25,)), S((4,)), S((6,)), S((6,)),
         S((16,)), S((16,)), S((16,)), S((16,)), S((16,)), S((16,)), S((4,)),
     ]
     return pl.pallas_call(
         k3_kernel,
         out_shape=[
-            sds((1024, D), BF), sds((4, 96, D), F32), sds((4, 16, FF), F32), sds((4, 80, D), F32), sds((4, 32, FF), F32),
+            sds((1024, D), BF), sds((2, 2, 8, 64, 384), BF), sds((2, 2, 8, 32, 384), BF),
         ],
-        in_specs=[ANY()] * 7 + [INV()] * 3 + [ANY()] * 6 + [INV()] * 2 + [ANY()],
-        out_specs=[ANY()] + [INV()] * 4,
+        in_specs=[ANY()] * 19,
+        out_specs=[ANY()] * 3,
         scratch_shapes=scratch + gather_sems(2),
         compiler_params=pltpu.CompilerParams(
             vmem_limit_bytes=VMEM_LIMIT, collective_id=2, has_side_effects=True
         ),
+    )(*args)
+
+
+def k4_call(*args):
+    V = pltpu.VMEM
+    grads = [(4, 96, D), (4, 16, FF), (4, 80, D), (4, 32, FF)]
+    return pl.pallas_call(
+        k4_kernel,
+        out_shape=[sds((1024, D), BF), sds((1024, D), BF)] + [sds(s, F32) for s in grads],
+        in_specs=[ANY()] * 4,
+        out_specs=[ANY()] * 6,
+        scratch_shapes=[V((2, 2, 8, 64, 384), BF), V((2, 2, 8, 32, 384), BF)]
+        + [V(s, F32) for s in grads]
+        + [V((1024, D), BF), V((1024, D), BF), pltpu.SemaphoreType.DMA((10,))],
+        compiler_params=pltpu.CompilerParams(vmem_limit_bytes=VMEM_LIMIT),
     )(*args)
 
 
@@ -1594,9 +1665,10 @@
         qkv_weight[0], out_weight[0], ffn_in_weight[0], ffn_out_weight[0],
     )
     q, k, v = (a.reshape(1536, D) for a in (q, k, v))
-    dx, g_in, g_dn, g_out, g_ff = k3_call(
+    dx, eg, lg = k3_call(
         x, q, k, v, p, do, hf, ge, gao, tag, lowq, done, cos, sin, fq, fk, aqkv, bqkv, wq
     )
+    mixed, dx, g_in, g_dn, g_out, g_ff = k4_call(eg, lg, mixed, dx)
     return (
         mixed[None], dx[None], g_in.reshape(ADAPTERS, 6, 16, D).transpose(0, 1, 3, 2)[None],
         g_dn.transpose(0, 2, 1)[None], g_out.reshape(ADAPTERS, 5, 16, D)[None], g_ff.reshape(ADAPTERS, 2, 16, FF)[None],

time: 271 us -> 258 us (0.952)
  local copies, waits for them, and re-layouts: 9.14 us -> 0 us
  Pallas kernels: 255 us -> 252 us
    pallas_call x1, Pallas kernels: 170 us -> 160 us  [kf_call(): pl.pallas_call(kf_kernel, out_shape=[sds(s, t) for _, s, t in outs], in_s...]
    unnamed x16 -> x0, local copies, waits for them, and re-layouts: 9.14 us -> none
    pallas_call x1 -> x2, Pallas kernels: 85.3 us -> 92.2 us  [the longest x1 86.4 us: k3_call(): pl.pallas_call(k3_kernel, out_shape=[sds((1024, D), BF), sds((2, 2, 8, 64...]
where the time goes in v2:
time: 258 us; the launch traced here: 254 us
  Pallas kernels  252 us (98%)
    pallas_call x1, Pallas kernels, kf_call(): pl.pallas_call(kf_kernel, out_shape=[sds(s, t) for _, s, t in outs], in_s...  160 us
    pallas_call x1, Pallas kernels, k3_call(): pl.pallas_call(k3_kernel, out_shape=[sds((1024, D), BF), sds((2, 2, 8, 64...  86.4 us
    pallas_call x1, Pallas kernels, k4_call(): pl.pallas_call(k4_kernel, out_shape=[sds((1024, D), BF), sds((1024, D), B...  5.79 us

profile of v2, /device:TPU:1, one launch (start us, length us, event | category | flops | bytes accessed | tf_op | source)
XLA Modules:
  0.0 253.8 jit_solution(2784077066070871980)
XLA Ops:
  1.3 159.8 %shard_map.190 = (bf16[6,256,768]{2,1,0:T(8,128)(2,1)}, bf16[6,256,768]{2,1,0:T(8,128)(2,1)}, bf16[6,256,768]{2,1,0:T(8,128)(2,1)}, bf16[4,6,4,256,768]{4,3,2,1,...) custom-call(bf16[1024,768]{1,0:T(8,128)(2,1)} %bitcast.33, ...), custom_call_target="tpu_custom_call" | custom-call | tf_op jit(solution)/shard_map/pallas_call | solution.py:1599
  161.1 86.4 %shard_map.191 = (bf16[1024,768]{1,0:T(8,128)(2,1)}, bf16[2,2,8,64,384]{4,3,2,1,0:T(8,128)(2,1)}, bf16[2,2,8,32,384]{4,3,2,1,0:T(8,128)(2,1)}) custom-call(bf16[1024,768]{1,0:T(8,128)(2,1)} %bitcast.34, bf16[1536,768]{1,0:T(8,128)(2,1)} %bitcast.35, bf16[1536,768]{1,0:T(8,128)(2,1)} %bitcast.36, bf16[1536,768]{1,0:T(8,128)(2,1)} %bitcast.37, ...), custom_call_target="tpu_custom_call" | custom-call | tf_op jit(solution)/shard_map/pallas_call | solution.py:1625
  247.5 5.8 %shard_map.192 = (bf16[1024,768]{1,0:T(8,128)(2,1)}, bf16[1024,768]{1,0:T(8,128)(2,1)}, f32[4,96,768]{2,1,0:T(8,128)}, f32[4,16,3072]{2,1,0:T(8,128)}, f32[4,80,768]{2,1,0:T(8,128)}, /*index=5*/f32[4,32,3072]{2,1,0:T(8,128)}) custom-call(bf16[2,2,8,64,384]{4,3,2,1,0:T(8,128)(2,1)} %get-tuple-element.52.eg_hbm, ...), custom_call_target="tpu_custom_call" | custom-call | tf_op jit(solution)/shard_map/pallas_call | solution.py:1642

commit v3 on v2

--- a/solution.py
+++ b/solution.py
@@ -743,13 +743,20 @@
     lane = iota((1, 128), 1)
     slot = lax.rem(step, 2)
 
-    def copy(s):
-        return prob_copies(n, stage.at[pl.ds(s * 4, 4)], p_hbm.at[qb, pair], sem, s)
+    def copy(s, tiles=n):
+        return prob_copies(tiles, stage.at[pl.ds(s * 4, 4)], p_hbm.at[qb, pair], sem, s)
 
     @pl.when(pair >= 2)
     def _():
         for one in copy(slot):
             one.wait()
+
+    if qb > 0:
+
+        @pl.when(pair < 2)
+        def _():
+            for one in copy(slot, PLAN[qb - 1][1]):
+                one.wait()
 
     lanes = pl.ds(pl.multiple_of(pair * 128, 128), 128)
     q2 = q_ref[qb, :, lanes]
@@ -790,6 +797,10 @@
             one.wait()
 
 
+def sigmoid(v):
+    return 0.5 * jnp.tanh(0.5 * v) + 0.5
+
+
 def norm_stats(r):
     centre = r - jnp.mean(r, axis=1, keepdims=True)
     rstd = lax.rsqrt(jnp.mean(centre * centre, axis=1, keepdims=True) + EPSILON)
@@ -830,12 +841,14 @@
         lanes = slice(c * 256, c * 256 + 256)
         gate = nn(act, wi[n, 0, :, :, :, :, lanes].reshape(D, 256)) + nn(low, bg[n, :, lanes])
         up = nn(act, wi[n, 1, :, :, :, :, lanes].reshape(D, 256)) + nn(low, bu[n, :, lanes])
-        parts.append((gate * (1.0 / (1.0 + jnp.exp(-gate))) * up).astype(BF))
+        parts.append((gate * sigmoid(gate) * up).astype(BF))
         big[pl.ds(here, blocks), :, lanes] = gate.astype(BF).reshape(blocks, QB, 256)
         big[pl.ds(here + 16, blocks), :, lanes] = up.astype(BF).reshape(blocks, QB, 256)
     inner = jnp.concatenate(parts, axis=1)
     lowd_ref[rows, 0:16] += nt(inner, adn[n])
-    total_ref[rows, :] += nn(inner, wd[lax.div(n, 2), lax.rem(n, 2)].reshape(D, D))
+    for c in range(3):
+        lanes = slice(c * 256, c * 256 + 256)
+        total_ref[rows, lanes] += nn(inner, wd[lax.div(n, 2), lax.rem(n, 2), :, :, lanes].reshape(D, 256))
 
 
 def ffn_out_rows(
@@ -871,14 +884,14 @@
         dinner = nt(db2, down[lanes]) + nn(dlow, adn[n, :, lanes])
         gate = big[pl.ds(here, blocks), :, lanes].reshape(size, 256).astype(F32)
         up = big[pl.ds(here + 16, blocks), :, lanes].reshape(size, 256).astype(F32)
-        sig = 1.0 / (1.0 + jnp.exp(-gate))
+        sig = sigmoid(gate)
         silu = gate * sig
         inners.append((silu * up).astype(BF))
         dgs.append((dinner * up * (sig + silu * (1.0 - sig))).astype(BF))
         dus.append((dinner * silu).astype(BF))
     dg, du, inner = (jnp.concatenate(v, axis=1) for v in (dgs, dus, inners))
     acc[...] += nt(dg, wi[n, 0].reshape(D, D)) + nt(du, wi[n, 1].reshape(D, D))
-    dlf_ref[...] += nt(dg, bg[n]) + nt(du, bu[n])
+    dlf_ref[...] += nt(bg[n], dg) + nt(bu[n], du)
     gadn_ref[n] += tn(dlow, inner)
     low = lowf_ref[rows, :]
     gbf_ref[n] += jnp.where(iota((32, 1), 0) < 16, tn(low, dg), tn(low, du))
@@ -891,7 +904,7 @@
     start = pl.multiple_of(rb * QB, QB)
     rows = pl.ds(start, QB)
     local = pl.ds(pl.multiple_of(start - off, QB), QB)
-    dlf = dlf_ref[local, :].astype(BF)
+    dlf = dlf_ref[:, local].T.astype(BF)
     dhid = dtwo_ref[rows, :] + acc[local, :] + nn(dlf, aff[...])
     gaff_ref[...] += tn(dlf, act_ref[rows, :])
     done = norm_back(dhid * gb[0:1, :], xhat_ref[rows, :], rstd_ref[rows, 0:1])
@@ -923,10 +936,12 @@
     ao, bo, aff, adn, bdn, gb,
     gaff_ref, gadn_ref, gbo_ref, gbdn_ref, gbf_ref,
     wq, wo, wi, wd, big, xw, att, linv, xhat, dtwo, act, db2, cos, sin, fq, fk, bias, mf,
-    lowq, lowo, lowf, dlow, acc, dlf, bblk, bg, bu, h2, mixed_ref, do_ref, rsem, tsem, wsem, xsem, osem, psem, hs, hr, *sems,
+    lowq, lowo, lowf, dlow, acc, dlf, bblk, bg, bu, h2, rsem, tsem, wsem, xsem, osem, psem, hs, hr, *sems,
 ):
     flip = lax.axis_index("seq")
     cot = db2
+    do_ref = db2
+    mixed_ref = xw.at[pl.ds(0, 1024)]
     rstd = cos
     lowd = sin
     loads = []
@@ -1071,7 +1086,7 @@
             return 0
 
         lax.fori_loop(first, last, pair_step, 0)
-        if last == 6:
+        if last == 6 and qb == 3:
             drain_pairs(qb, p_hbm, stage, psem)
 
     def out_step(rb, _):
@@ -1079,7 +1094,7 @@
         return 0
 
     def in_step(i, _):
-        ffn_in_tile(lax.div(i, 2), lax.rem(i, 2), 512, act, lowf, wi, wd, bg, bu, adn, big, lowd, dtwo)
+        ffn_in_tile(i, 0, 1024, act, lowf, wi, wd, bg, bu, adn, big, lowd, dtwo)
         return 0
 
     for step in ORDER:
@@ -1109,7 +1124,7 @@
             lax.fori_loop(0, 4, out_step, 0)
         elif kind == "F":
             n = int(rest)
-            lax.fori_loop(2 * n, 2 * n + 2, in_step, 0)
+            lax.fori_loop(n, n + 1, in_step, 0)
 
     def down_step(rb, _):
         ffn_out_rows(rb, flip, lowd, bdn, xhat, gb, cot, dtwo, db2, dlow, mixed_ref, gbdn_ref)
@@ -1200,7 +1215,14 @@
                 x_hbm.at[pl.ds(block_at(flip, i), QB)], xw.at[pl.ds(i * QB, QB)], sem.at[21 + i]
             )
         )
-    for copy in loads:
+    def fetch(qb, pair, s):
+        return prob_copies(PLAN[qb][1], p_hbm.at[qb, pair], stage.at[s], psem, s)
+
+    for copy in loads[:5]:
+        copy.start()
+    for copy in fetch(0, 0, 0):
+        copy.start()
+    for copy in loads[5:]:
         copy.start()
 
     def view(c, za, zb, k, half):
@@ -1259,7 +1281,6 @@
     lax.fori_loop(1, 16, greet, 0)
     for dev in (g.devy, g.devd):
         pl.semaphore_signal(bar, inc=1, device_id=dev, device_id_type=MESH)
-    pl.semaphore_wait(bar, 17)
     halo = []
     for i, (src, dst) in enumerate(
         (
@@ -1276,9 +1297,6 @@
                 src, dst, hs.at[i], hr.at[i], device_id=g.devy, device_id_type=MESH
             )
         )
-    for copy in (halo[4], halo[0], halo[1], halo[2], halo[3]):
-        copy.start()
-    send_t()
 
     def total_of(ref):
         totals = [0.0] * ADAPTERS
@@ -1315,21 +1333,23 @@
         rows = pl.ds(qb * QB, QB)
         krows = pl.ds(k0 * QB, n * QB)
 
-        def fetch(pair, s, qb=qb, n=n):
-            return prob_copies(n, p_hbm.at[qb, pair], stage.at[s], psem, s)
-
-        for one in fetch(0, 0):
-            one.start()
-
-        def pair_step(pair, _, k0=k0, n=n, own=own, rows=rows, krows=krows, fetch=fetch):
+
+        def pair_step(pair, _, qb=qb, k0=k0, n=n, own=own, rows=rows, krows=krows):
             slot = lax.rem(pair, 2)
-            for one in fetch(pair, slot):
+            for one in fetch(qb, pair, slot):
                 one.wait()
 
             @pl.when(pair < 5)
             def _():
-                for one in fetch(pair + 1, 1 - slot):
+                for one in fetch(qb, pair + 1, 1 - slot):
                     one.start()
+
+            if qb < 3:
+
+                @pl.when(pair == 5)
+                def _():
+                    for one in fetch(qb + 1, 0, 0):
+                        one.start()
 
             lanes = pl.ds(pl.multiple_of(pair * 128, 128), 128)
             do2 = do[rows, lanes]
@@ -1356,23 +1376,26 @@
 
         lax.fori_loop(0, 6, pair_step, 0)
         if qb == 0:
+            pl.semaphore_wait(bar, 17)
+            for copy in (halo[4], halo[0], halo[1], halo[2], halo[3]):
+                copy.start()
+            send_t()
+            for copy in loads[5:9]:
+                copy.wait()
+        elif qb == 1:
             halo[4].wait_recv()
             mine = ge[pl.ds(pl.multiple_of(flip * 128, 16), 128), :]
             e_half[...] = (mine.astype(F32) + e_in[...].astype(F32)).astype(BF)
             send_e()
-            for copy in loads[5:9]:
-                copy.wait()
-        elif qb == 1:
+        elif qb == 2:
             rs_e[g.b] = own_piece(e_half, 16)
             rs_t[g.b] = tag[...]
             wait_e()
             wait_t()
             eg[g.za, g.zb, g.column(0, 0, 0)] = total_of(rs_e)
             g.send_z(0)
-        elif qb == 2:
+        else:
             g.stage_z(0)
-        else:
-            g.stage_xy(0)
 
     for copy in loads[11:]:
         copy.wait()
@@ -1413,9 +1436,9 @@
         return 0
 
     lax.fori_loop(0, 3, halo_step, 0)
+    g.stage_xy(0)
+    lax.fori_loop(3, 6, halo_step, 0)
     g.stage_corner(0)
-    lax.fori_loop(3, 6, halo_step, 0)
-    g.stage_pair(0)
 
     lane = lax.div(iota((1, 48), 1), 16)
     rank = lax.div(iota((48, 1), 0), 16)
@@ -1432,7 +1455,10 @@
                 d = rope(dq[rows, :], cosine, sine)
             else:
                 src = (dkT, dvT)[p - 1]
-                d = jnp.concatenate([src[pl.ds(c * 128, 128), rows].T for c in range(6)], axis=1)
+                d = [src[pl.ds(c * 128, 128), rows] for c in range(6)]
+                if p == 2:
+                    d = [v.astype(BF) for v in d]
+                d = jnp.concatenate([v.T for v in d], axis=1)
                 if p == 1:
                     d = rope(d, cosine, sine)
             d = d.astype(BF)
@@ -1445,6 +1471,7 @@
         return 0
 
     lax.fori_loop(0, 4, proj_step, 0)
+    g.stage_pair(0)
     gl_out[0:48] = ga_ref[...].astype(BF)
     gl_out[48:96] = gbq_ref[...].astype(BF)
     gl_out[96:112] = gao[...].astype(BF)
@@ -1590,8 +1617,8 @@
         V((1024, D), F32), V((1024, D), F32), V((1024, D), BF), V((1024, D), BF),
         V((1536, 128), F32), V((1536, 128), F32), V((1536, 128), BF), V((1536, 128), BF), V((2, QB, QB), F32),
         V((1024, 128), F32), V((1536, 48), BF), V((1024, 16), BF), V((1024, 32), BF),
-        V((1024, 16), BF), V((512, D), F32), V((512, 32), F32), V((3, 48, D), BF),
-        V((4, 32, D), BF), V((4, 32, D), BF), V((D, 128), BF), V((1024, D), BF), V((1024, D), BF),
+        V((1024, 16), BF), V((512, D), F32), V((32, 512), F32), V((3, 48, D), BF),
+        V((4, 32, D), BF), V((4, 32, D), BF), V((D, 128), BF),
         pltpu.SemaphoreType.DMA((13,)), pltpu.SemaphoreType.DMA((10,)), pltpu.SemaphoreType.DMA((7,)), pltpu.SemaphoreType.DMA((8,)), pltpu.SemaphoreType.DMA((10,)),
         pltpu.SemaphoreType.DMA((4,)), pltpu.SemaphoreType.DMA((4,)), pltpu.SemaphoreType.DMA((4,)),
     ]

time: 258 us -> 253 us (0.981)
  Pallas kernels: 252 us -> 247 us
    pallas_call x1, Pallas kernels: 86.4 us -> 81.8 us  [k3_call(): pl.pallas_call(k3_kernel, out_shape=[sds((1024, D), BF), sds((2, 2, 8, 64...]
where the time goes in v3:
time: 253 us; the launch traced here: 248 us
  Pallas kernels  247 us (98%)
    pallas_call x1, Pallas kernels, kf_call(): pl.pallas_call(kf_kernel, out_shape=[sds(s, t) for _, s, t in outs], in_s...  159 us
    pallas_call x1, Pallas kernels, k3_call(): pl.pallas_call(k3_kernel, out_shape=[sds((1024, D), BF), sds((2, 2, 8, 64...  81.8 us
    pallas_call x1, Pallas kernels, k4_call(): pl.pallas_call(k4_kernel, out_shape=[sds((1024, D), BF), sds((1024, D), B...  5.79 us

profile of v3, /device:TPU:1, one launch (start us, length us, event | category | flops | bytes accessed | tf_op | source)
XLA Modules:
  0.0 248.2 jit_solution(9648780986905958930)
XLA Ops:
  1.3 159.0 %shard_map.190 = (bf16[6,256,768]{2,1,0:T(8,128)(2,1)}, bf16[6,256,768]{2,1,0:T(8,128)(2,1)}, bf16[6,256,768]{2,1,0:T(8,128)(2,1)}, bf16[4,6,4,256,768]{4,3,2,1,...) custom-call(bf16[1024,768]{1,0:T(8,128)(2,1)} %bitcast.33, ...), custom_call_target="tpu_custom_call" | custom-call | tf_op jit(solution)/shard_map/pallas_call | solution.py:1626
  160.3 81.8 %shard_map.191 = (bf16[1024,768]{1,0:T(8,128)(2,1)}, bf16[2,2,8,64,384]{4,3,2,1,0:T(8,128)(2,1)}, bf16[2,2,8,32,384]{4,3,2,1,0:T(8,128)(2,1)}) custom-call(bf16[1024,768]{1,0:T(8,128)(2,1)} %bitcast.34, bf16[1536,768]{1,0:T(8,128)(2,1)} %bitcast.35, bf16[1536,768]{1,0:T(8,128)(2,1)} %bitcast.36, bf16[1536,768]{1,0:T(8,128)(2,1)} %bitcast.37, ...), custom_call_target="tpu_custom_call" | custom-call | tf_op jit(solution)/shard_map/pallas_call | solution.py:1652
  242.1 5.8 %shard_map.192 = (bf16[1024,768]{1,0:T(8,128)(2,1)}, bf16[1024,768]{1,0:T(8,128)(2,1)}, f32[4,96,768]{2,1,0:T(8,128)}, f32[4,16,3072]{2,1,0:T(8,128)}, f32[4,80,768]{2,1,0:T(8,128)}, /*index=5*/f32[4,32,3072]{2,1,0:T(8,128)}) custom-call(bf16[2,2,8,64,384]{4,3,2,1,0:T(8,128)(2,1)} %get-tuple-element.52.eg_hbm, ...), custom_call_target="tpu_custom_call" | custom-call | tf_op jit(solution)/shard_map/pallas_call | solution.py:1669

commit v4 on v3

--- a/solution.py
+++ b/solution.py
@@ -816,14 +816,14 @@
 
 
 def out_rows(rb, xw, att_ref, wo, ao, bo, gb, aff, xhat_ref, rstd_ref, act_ref, lowo_ref, lowf_ref):
-    rows = pl.ds(pl.multiple_of(rb * QB, QB), QB)
+    rows = pl.ds(pl.multiple_of(rb * 512, 512), 512)
     att = att_ref[rows, :]
     low = nt(att, ao[...]).astype(BF)
     lowo_ref[rows, :] = low
     branch = nn(att, wo[...].reshape(D, D)) + nn(low, bo[...])
     xhat, rstd = norm_stats(xw[rows, :].astype(F32) + branch)
     xhat_ref[rows, :] = xhat
-    rstd_ref[rows, :] = jnp.broadcast_to(rstd, (QB, 128))
+    rstd_ref[rows, :] = jnp.broadcast_to(rstd, (512, 128))
     act = (xhat * gb[0:1, :] + gb[1:2, :]).astype(BF)
     act_ref[rows, :] = act
     lowf_ref[rows, :] = nt(act, aff[...]).astype(BF)
@@ -1121,7 +1121,7 @@
             for copy in saves:
                 copy.wait()
             lowd[...] = jnp.zeros_like(lowd)
-            lax.fori_loop(0, 4, out_step, 0)
+            lax.fori_loop(0, 2, out_step, 0)
         elif kind == "F":
             n = int(rest)
             lax.fori_loop(n, n + 1, in_step, 0)
@@ -1444,12 +1444,12 @@
     rank = lax.div(iota((48, 1), 0), 16)
 
     def proj_step(rb, _):
-        start = pl.multiple_of(rb * QB, QB)
-        rows = pl.ds(start, QB)
+        start = pl.multiple_of(rb * 512, 512)
+        rows = pl.ds(start, 512)
         cosine = cos[rows, :]
         sine = -sin[rows, :]
         low = lowq[rows, :]
-        dlow = jnp.zeros((QB, 48), F32)
+        dlow = jnp.zeros((512, 48), F32)
         for p in range(3):
             if p == 0:
                 d = rope(dq[rows, :], cosine, sine)
@@ -1470,7 +1470,7 @@
         ga_ref[...] += tn(dlow, xw[rows, :])
         return 0
 
-    lax.fori_loop(0, 4, proj_step, 0)
+    lax.fori_loop(0, 2, proj_step, 0)
     g.stage_pair(0)
     gl_out[0:48] = ga_ref[...].astype(BF)
     gl_out[48:96] = gbq_ref[...].astype(BF)

time: 253 us -> 251 us (level)
  no operation moved by 1% of the time
where the time goes in v4:
time: 251 us; the launch traced here: 247 us
  Pallas kernels  245 us (98%)
    pallas_call x1, Pallas kernels, kf_call(): pl.pallas_call(kf_kernel, out_shape=[sds(s, t) for _, s, t in outs], in_s...  158 us
    pallas_call x1, Pallas kernels, k3_call(): pl.pallas_call(k3_kernel, out_shape=[sds((1024, D), BF), sds((2, 2, 8, 64...  81.4 us
    pallas_call x1, Pallas kernels, k4_call(): pl.pallas_call(k4_kernel, out_shape=[sds((1024, D), BF), sds((1024, D), B...  5.79 us

profile of v4, /device:TPU:1, one launch (start us, length us, event | category | flops | bytes accessed | tf_op | source)
XLA Modules:
  0.0 246.7 jit_solution(1996986386639113203)
XLA Ops:
  1.3 157.8 %shard_map.190 = (bf16[6,256,768]{2,1,0:T(8,128)(2,1)}, bf16[6,256,768]{2,1,0:T(8,128)(2,1)}, bf16[6,256,768]{2,1,0:T(8,128)(2,1)}, bf16[4,6,4,256,768]{4,3,2,1,...) custom-call(bf16[1024,768]{1,0:T(8,128)(2,1)} %bitcast.33, ...), custom_call_target="tpu_custom_call" | custom-call | tf_op jit(solution)/shard_map/pallas_call | solution.py:1626
  159.1 81.4 %shard_map.191 = (bf16[1024,768]{1,0:T(8,128)(2,1)}, bf16[2,2,8,64,384]{4,3,2,1,0:T(8,128)(2,1)}, bf16[2,2,8,32,384]{4,3,2,1,0:T(8,128)(2,1)}) custom-call(bf16[1024,768]{1,0:T(8,128)(2,1)} %bitcast.34, bf16[1536,768]{1,0:T(8,128)(2,1)} %bitcast.35, bf16[1536,768]{1,0:T(8,128)(2,1)} %bitcast.36, bf16[1536,768]{1,0:T(8,128)(2,1)} %bitcast.37, ...), custom_call_target="tpu_custom_call" | custom-call | tf_op jit(solution)/shard_map/pallas_call | solution.py:1652
  240.5 5.8 %shard_map.192 = (bf16[1024,768]{1,0:T(8,128)(2,1)}, bf16[1024,768]{1,0:T(8,128)(2,1)}, f32[4,96,768]{2,1,0:T(8,128)}, f32[4,16,3072]{2,1,0:T(8,128)}, f32[4,80,768]{2,1,0:T(8,128)}, /*index=5*/f32[4,32,3072]{2,1,0:T(8,128)}) custom-call(bf16[2,2,8,64,384]{4,3,2,1,0:T(8,128)(2,1)} %get-tuple-element.52.eg_hbm, ...), custom_call_target="tpu_custom_call" | custom-call | tf_op jit(solution)/shard_map/pallas_call | solution.py:1669
